TPU v7x, 512 devices: a whole 4x4x16 slice. The times are simulated.
512 devices in a mesh: seq: 64 (over y, z), head: 8 (over x, core).
Axes of the slice: x: 4, y: 4, z: 16, core: 2. Of those that a mesh axis runs over, the one named last changes fastest.
Arguments:
- queries: bfloat16 [32768, 4096], P('seq', 'head'), may hold values from -6 to 6
- keys: bfloat16 [32768, 4096], P('seq', 'head'), may hold values from -6 to 6
- values: bfloat16 [32768, 4096], P('seq', 'head'), may hold values from -6 to 6
- out_weight: bfloat16 [4096, 4096], P('head', 'seq'), may hold values from -0.09375 to 0.09375
- head_gain: float32 [4096], P('head'), may hold values from 0.1 to 1.9
Outputs:
- layer_out: bfloat16 [32768, 4096], P(('seq', 'head'))
All inputs are finite; a program needn't handle non-finite values.
Results may differ from a plain program's by a relative error of at most 0.017.
Values may be sent and summed in bfloat16 or wider, within the bound.
No kernel may reach another device: no remote copies, remote signals or barrier semaphores. Data moves between devices by JAX's collectives and lax.ppermute only.
A program may use at most 64 MiB of HBM per device.

v0:
```python
import jax
import jax.numpy as jnp
from jax import lax
from jax.sharding import PartitionSpec as P

DH = 128


def carried_in(value, axis, join, neutral):
    count, mine = (lax.axis_size(axis), lax.axis_index(axis))
    pieces = lax.all_gather(value, axis)
    subtotal = jnp.full_like(value, 0) + jnp.asarray(neutral, value.dtype)

    def lap(position, subtotal):
        longer = join(subtotal, pieces[position])
        return jnp.where(position < mine, longer, subtotal)

    return lax.fori_loop(0, count - 1, lap, subtotal)


def feature(inputs):
    return jax.nn.elu(inputs.astype(jnp.float32)) + 1.0


def add_memory(earlier, later):
    return earlier + later


def body(queries, keys, values, out_weight, head_gain):
    highest = lax.Precision.HIGHEST
    row_count = queries.shape[0]
    local_heads = queries.shape[1] // DH
    query_bf = feature(queries).astype(jnp.bfloat16).reshape(row_count, local_heads, DH)
    key_bf = feature(keys).astype(jnp.bfloat16).reshape(row_count, local_heads, DH)
    value_bf = values.reshape(row_count, local_heads, DH)
    memory = jnp.einsum("thd,the->hde", key_bf, value_bf, preferred_element_type=jnp.float32)
    empty_memory = jnp.zeros_like(memory)
    prior_memory = carried_in(memory, "seq", add_memory, empty_memory)
    query_exact = query_bf.astype(jnp.float32)
    numerator = jnp.einsum("thd,hde->the", query_exact, prior_memory, precision=highest)
    causal = jnp.tril(jnp.ones((row_count, row_count), dtype=bool))
    scores = jnp.einsum("thd,shd->hts", query_bf, key_bf, preferred_element_type=jnp.float32)
    scores = jnp.where(causal[None, :, :], scores, 0.0)
    weights = scores.astype(jnp.bfloat16)
    attended = numerator + jnp.einsum(
        "hts,she->the", weights, value_bf, preferred_element_type=jnp.float32
    )
    mean_square = jnp.mean(attended * attended, axis=-1, keepdims=True)
    gain_heads = head_gain.reshape(local_heads, DH)
    normed = (attended * lax.rsqrt(mean_square + 1e-05) * gain_heads[None]).astype(jnp.bfloat16)
    normed = normed.reshape(row_count, local_heads * DH)
    weight_rows = lax.all_gather(out_weight, "seq", axis=1, tiled=True)
    return lax.psum_scatter(
        jnp.dot(normed, weight_rows, preferred_element_type=jnp.float32).astype(jnp.bfloat16),
        "head",
        scatter_dimension=0,
        tiled=True,
    )


def solution(mesh):
    placed = (P("seq", "head"), P("seq", "head"), P("seq", "head"), P("head", "seq"), P("head"))
    return jax.shard_map(
        body, mesh=mesh, in_specs=placed, out_specs=P(("seq", "head"), None), check_vma=False
    )
```

profile of v0, /device:TPU:24, one launch (start us, length us, event | category | flops | bytes accessed | tf_op | source)
XLA Modules:
  0.0 407.7 jit_solution(1077520196212806162)
XLA Ops:
  6.5 1.5 fusion.5
  8.3 1.3 copy.18
  11.5 195.0 %all-gather.6.cloned.1.call-done = f32[256,128,128]{2,1,0:T(8,128)} async-done(((f32[4,128,128]{2,1,0:T(8,128)}), f32[256,128,128]{2,1,0:T(8,128)}) %all-gather.6.cloned.1.call-update) | async-done | bytes 16777232 | tf_op jit(solution)/shard_map/all_gather | solution.py:11
  206.5 67.0 %while.14 = (s32[]{:T(128)}, f32[4,128,128]{2,1,0:T(8,128)S(1)}, s32[]{:T(128)}, f32[64,4,128,128]{3,2,1,0:T(8,128)}, s32[]{:T(128)}, /*index=5*/s32[]{:T(128)}) while((s32[]{:T(128)}, f32[4,128,128]{2,1,0:T(8,128)S(1)}, s32[]{:T(128)}, f32[64,4,128,128]{3,2,1,0:T(8,128)}, s32[]{:T(128)}, /*index=5*/s32[]{:T(128)}) %tuple.42), condition=%wide.region_1.2_spmd.clone, body=%wide.region_0.1_spmd.clone.sunk | while | flops 196612 | bytes 786525 | solution.py:18
  208.6 1.0 add_select_fusion.2
  210.8 1.0 add_select_fusion.2
  212.9 1.0 add_select_fusion.2
  215.0 1.0 add_select_fusion.2
  217.2 1.0 add_select_fusion.2
  229.9 1.0 add_select_fusion.2
  233.1 1.0 add_select_fusion.2
  237.4 1.0 add_select_fusion.2
  240.6 1.0 add_select_fusion.2
  244.8 1.0 add_select_fusion.2
  248.0 1.0 add_select_fusion.2
  259.7 1.0 add_select_fusion.2
  261.9 1.0 add_select_fusion.2
  265.1 1.0 add_select_fusion.2
  268.2 1.0 add_select_fusion.2
  273.6 1.9 convolution_bitcast_fusion
  275.5 2.7 multiply_reduce_fusion
  278.4 73.9 %all-gather.4.cloned.1.call-done = bf16[512,4096]{0,1:T(8,128)(2,1)} async-done(((bf16[512,64]{0,1:T(8,128)(2,1)}), bf16[512,4096]{0,1:T(8,128)(2,1)}) %all-gather.4.cloned.1.call-update) | async-done | bytes 4194320 | tf_op jit(solution)/shard_map/all_gather | solution.py:52
  352.3 6.5 %convolution_convert_fusion = bf16[512,4096]{1,0:T(8,128)(2,1)} fusion(bf16[512,512]{0,1:T(8,128)(2,1)S(1)} %bitcast.41, bf16[512,4096]{0,1:T(8,128)(2,1)} %all-gather.4.cloned.1.call-done), kind=kOutput, calls=%fused_computation.1 | convolution fusion | flops 2149580800 | bytes 8912896 | tf_op jit(solution)/shard_map/dot_general | solution.py:54
  358.8 42.4 %reduce-scatter.2.cloned.1.call-done = bf16[64,4096]{1,0:T(8,128)(2,1)} async-done(((bf16[512,4096]{1,0:T(8,128)(2,1)}), bf16[64,4096]{1,0:T(8,128)(2,1)}) %reduce-scatter.2.cloned.1.call-update) | async-done | bytes 524304 | tf_op jit(solution)/shard_map/reduce_scatter | solution.py:53
  (64 shorter events, 52.2 us)
Async XLA Ops:
  6.5 200.0 %all-gather.6.cloned.1.call-start = ((), (), s32[]{:S(2)}) async-start(), calls=%async_computation.3 | async-start | bytes 17039360 | tf_op jit(solution)/shard_map/all_gather | solution.py:11
  8.0 265.5 %copy-start.1 = (bf16[512,512]{1,0:T(8,128)(2,1)S(1)}, bf16[512,512]{1,0:T(8,128)(2,1)}, u32[]{:S(2)}) copy-start(bf16[512,512]{1,0:T(8,128)(2,1)} %param.7) | copy-start | bytes 1572868
  10.6 341.7 %all-gather.4.cloned.1.call-start = ((), (), s32[]{:S(2)}) async-start(), calls=%async_computation.1 | async-start | bytes 4259840 | tf_op jit(solution)/shard_map/all_gather | solution.py:52
  11.3 389.9 %reduce-scatter.2.cloned.1.call-start = ((), (), s32[]{:S(2)}) async-start(), calls=%async_computation.2 | async-start | bytes 4718592 | tf_op jit(solution)/shard_map/reduce_scatter | solution.py:53
  275.5 2.7 copy-start
Sparse Core Ops, SparseCore 0:
  10.7 195.7 all-gather.5
  209.5 142.7 all-gather.3
  358.9 42.1 reduce-scatter.1
where the time goes:
time: 410 us; the launch traced here: 408 us
  waiting for transfers between devices  312 us (76%)
  other arithmetic  67.3 us (16%)
  between operations  13.2 us (3%)
  matrix products  12.2 us (3%)
    all_gather x1, waiting for transfers between devices, carried_in(): pieces = lax.all_gather(value, axis)  195 us
    all_gather x1, waiting for transfers between devices, body(): weight_rows = lax.all_gather(out_weight, 'seq', axis=1, tiled=True)  73.9 us
    select_n x63, other arithmetic, lap(): return jnp.where(position < mine, longer, subtotal)  65.6 us
    reduce_scatter x1, waiting for transfers between devices, body(): lax.psum_scatter(jnp.dot(normed, weight_rows, preferred_element_type=jnp....  42.4 us
  transfers between devices with their start and end apart: 3, of which 3 were waited for; matrix products, arithmetic and copies ran while one was open for 17% of the time, Pallas kernels for 0%

commit v1 on v0

v1 whole, which is shorter than its diff:
```python
import functools

import jax
import jax.numpy as jnp
from jax import lax
from jax.experimental import pallas as pl
from jax.experimental.pallas import tpu as pltpu
from jax.sharding import PartitionSpec as P

DH = 128
NY, NZ = 4, 16
Y_GROUPS = [[y * NZ + z for y in range(NY)] for z in range(NZ)]
Z_GROUPS = [[y * NZ + z for z in range(NZ)] for y in range(NY)]


def feature(inputs):
    return jax.nn.elu(inputs.astype(jnp.float32)) + 1.0


def prior_of(memory):
    count = lax.axis_size("seq")
    shape = memory.shape
    pieces = memory.astype(jnp.bfloat16).reshape(-1, DH)
    pieces = lax.all_to_all(pieces, "seq", 0, 0, tiled=True)
    earlier = jnp.tril(jnp.ones((count, count), jnp.bfloat16), -1)
    sums = jnp.dot(earlier, pieces.reshape(count, -1), preferred_element_type=jnp.float32)
    sums = sums.astype(jnp.bfloat16).reshape(-1, DH)
    return lax.all_to_all(sums, "seq", 0, 0, tiled=True).reshape(shape)


def project_kernel(normed_ref, weight_ref, out_ref):
    zs, _, cols, depth = weight_ref.shape
    weight = weight_ref[...].reshape(zs * cols, depth)
    out_ref[...] = lax.dot_general(
        normed_ref[...], weight, (((1,), (1,)), ((), ())), preferred_element_type=jnp.float32
    ).astype(out_ref.dtype)


def project(normed, weight):
    rows, depth = normed.shape
    _, _, cols, _ = weight.shape
    zs = 8
    return pl.pallas_call(
        project_kernel,
        grid=(NY, NZ // zs),
        in_specs=[
            pl.BlockSpec((rows, depth), lambda y, z: (0, 0)),
            pl.BlockSpec((zs, 1, cols, depth), lambda y, z: (z, y, 0, 0)),
        ],
        out_specs=pl.BlockSpec((rows, zs * cols), lambda y, z: (0, y * (NZ // zs) + z)),
        out_shape=jax.ShapeDtypeStruct((rows, NY * NZ * cols), jnp.bfloat16),
        compiler_params=pltpu.CompilerParams(vmem_limit_bytes=32 * 1024 * 1024),
        cost_estimate=pl.CostEstimate(
            flops=2 * rows * depth * NY * NZ * cols, bytes_accessed=9 << 20, transcendentals=0
        ),
    )(normed, weight)


def body(queries, keys, values, out_weight, head_gain):
    row_count = queries.shape[0]
    local_heads = queries.shape[1] // DH
    weight_t = lax.all_gather(out_weight.T, "seq", axis=0, tiled=True, axis_index_groups=Y_GROUPS)
    weight_t, keys, values = lax.optimization_barrier((weight_t, keys, values))
    weight_t = lax.all_gather(weight_t, "seq", axis=0, tiled=True, axis_index_groups=Z_GROUPS)
    query_bf = feature(queries).astype(jnp.bfloat16).reshape(row_count, local_heads, DH)
    key_bf = feature(keys).astype(jnp.bfloat16).reshape(row_count, local_heads, DH)
    value_bf = values.reshape(row_count, local_heads, DH)
    memory = jnp.einsum("thd,the->hde", key_bf, value_bf, preferred_element_type=jnp.float32)
    prior = prior_of(memory)
    numerator = jnp.einsum("thd,hde->the", query_bf, prior, preferred_element_type=jnp.float32)
    causal = jnp.tril(jnp.ones((row_count, row_count), dtype=bool))
    scores = jnp.einsum("thd,shd->hts", query_bf, key_bf, preferred_element_type=jnp.float32)
    scores = jnp.where(causal[None, :, :], scores, 0.0)
    weights = scores.astype(jnp.bfloat16)
    attended = numerator + jnp.einsum(
        "hts,she->the", weights, value_bf, preferred_element_type=jnp.float32
    )
    mean_square = jnp.mean(attended * attended, axis=-1, keepdims=True)
    gain_heads = head_gain.reshape(local_heads, DH)
    normed = (attended * lax.rsqrt(mean_square + 1e-05) * gain_heads[None]).astype(jnp.bfloat16)
    normed = normed.reshape(row_count, local_heads * DH)
    partial = project(normed, weight_t.reshape(NZ, NY, -1, weight_t.shape[-1]))
    return lax.psum_scatter(partial, "head", scatter_dimension=0, tiled=True)


def solution(mesh):
    placed = (P("seq", "head"), P("seq", "head"), P("seq", "head"), P("head", "seq"), P("head"))
    return jax.shard_map(
        body, mesh=mesh, in_specs=placed, out_specs=P(("seq", "head"), None), check_vma=False
    )
```

time: 410 us -> 168 us (0.41)
  waiting for transfers between devices: 312 us -> 97.6 us
  other arithmetic: 67.3 us -> 1.76 us
  starting transfers between devices: 0.08 us -> 21.1 us
  blocking collectives: 0 us -> 17.1 us
  matrix products: 12.2 us -> 5.48 us
  local copies, waits for them, and re-layouts: 1.48 us -> 6.49 us
  Pallas kernels: 0 us -> 4.36 us
    all_gather x2 -> x1, waiting for transfers between devices: 269 us -> 24.4 us  [body(): lax.all_gather(weight_t, 'seq', axis=0, tiled=True, axis_index_groups=Z_G...]
    select_n x63 -> x0, other arithmetic: 65.6 us -> none  [lap(): return jnp.where(position < mine, longer, subtotal)]
    all_to_all x0 -> x2, waiting for transfers between devices: none -> 31 us  [the longest x1 15.6 us: prior_of(): pieces = lax.all_to_all(pieces, 'seq', 0, 0, tiled=True)]
    all_to_all x0 -> x2, starting transfers between devices: none -> 21 us  [the longest x1 14.7 us: prior_of(): pieces = lax.all_to_all(pieces, 'seq', 0, 0, tiled=True)]
    all_gather x0 -> x1, blocking collectives: none -> 17.1 us  [body(): lax.all_gather(out_weight.T, 'seq', axis=0, tiled=True, axis_index_groups...]
    dot_general x2, matrix products: 8.47 us -> 1.84 us  [the longest x1 1.62 us: body(): jnp.einsum('thd,hde->the', query_bf, prior, preferred_element_type=jnp.fl...]
    unnamed x4 -> x9, local copies, waits for them, and re-layouts: 0.01 us -> 4.81 us
    pallas_call x0 -> x1, Pallas kernels: none -> 4.36 us  [project(): pl.pallas_call(project_kernel, grid=(NY, NZ // zs), in_specs=[pl.BlockSpe...]
  transfers between devices with their start and end apart: 3 -> 4, of which waited for: 3 -> 4; matrix products, arithmetic and copies ran while one was open for 17% -> 6% of each run, Pallas kernels for 0% -> 0%
where the time goes in v1:
time: 168 us; the launch traced here: 167 us
  waiting for transfers between devices  97.6 us (58%)
  starting transfers between devices  21.1 us (13%)
  blocking collectives  17.1 us (10%)
  between operations  13.5 us (8%)
  local copies, waits for them, and re-layouts  6.49 us (4%)
  matrix products  5.48 us (3%)
  Pallas kernels  4.36 us (3%)
  other arithmetic  1.76 us (1%)
    reduce_scatter x1, waiting for transfers between devices, body(): return lax.psum_scatter(partial, 'head', scatter_dimension=0, tiled=True)  42.2 us
    all_gather x1, waiting for transfers between devices, body(): lax.all_gather(weight_t, 'seq', axis=0, tiled=True, axis_index_groups=Z_G...  24.4 us
    all_gather x1, blocking collectives, body(): lax.all_gather(out_weight.T, 'seq', axis=0, tiled=True, axis_index_groups...  17.1 us
    all_to_all x1, waiting for transfers between devices, prior_of(): pieces = lax.all_to_all(pieces, 'seq', 0, 0, tiled=True)  15.6 us
    all_to_all x1, waiting for transfers between devices, prior_of(): return lax.all_to_all(sums, 'seq', 0, 0, tiled=True).reshape(shape)  15.4 us
    all_to_all x1, starting transfers between devices, prior_of(): pieces = lax.all_to_all(pieces, 'seq', 0, 0, tiled=True)  14.7 us
    all_to_all x1, starting transfers between devices, prior_of(): return lax.all_to_all(sums, 'seq', 0, 0, tiled=True).reshape(shape)  6.3 us
    unnamed x9, local copies, waits for them, and re-layouts  4.81 us
  transfers between devices with their start and end apart: 4, of which 4 were waited for; matrix products, arithmetic and copies ran while one was open for 6% of the time, Pallas kernels for 0%

profile of v1, /device:TPU:24, one launch (start us, length us, event | category | flops | bytes accessed | tf_op | source)
XLA Modules:
  0.0 167.3 jit_solution(14171503370089430389)
XLA Ops:
  6.5 17.1 %all_gather.6 = bf16[256,512]{1,0:T(8,128)(2,1)} all-gather(bf16[64,512]{1,0:T(8,128)(2,1)} %bitcast.45), channel_id=1, replica_groups={{0,128,256,384},{8,136,264,392},{16,144,272,400},{24,152,280,408},{32,1..., dimensions={0}, use_global_device_ids=true | all-gather | bytes 327680 | tf_op jit(solution)/shard_map/all_gather | solution.py:62
  23.7 0.0 all-gather.2.cloned.1.call-update
  23.7 1.5 fusion.6
  25.2 0.2 copy.18
  25.4 1.3 copy.20
  26.7 1.0 convolution_convert_fusion
  27.7 14.7 %all-to-all-start = ((bf16[64,8,128]{2,1,0:T(8,128)(2,1)}), bf16[64,8,128]{2,1,0:T(8,128)(2,1)S(1)}, u32[]{:S(2)}, u32[]{:S(2)}) async-start(bf16[64,8,128]{2,1,0:T(8,128)(2,1)} %bitcast.2), calls=%async_computation | async-start | bytes 262144 | tf_op jit(solution)/shard_map/all_to_all | solution.py:24
  42.4 15.6 %all-to-all-done = bf16[64,8,128]{2,1,0:T(8,128)(2,1)S(1)} async-done(((bf16[64,8,128]{2,1,0:T(8,128)(2,1)}), bf16[64,8,128]{2,1,0:T(8,128)(2,1)S(1)}, u32[]{:S(2)}, u32[]{:S(2)}) %all-to-all-start) | async-done | bytes 131104 | tf_op jit(solution)/shard_map/all_to_all | solution.py:24
  58.0 0.2 fusion.3
  58.2 0.7 copy.23
  58.9 6.3 %all-to-all-start.1 = ((bf16[64,8,128]{2,1,0:T(8,128)(2,1)}), bf16[64,8,128]{2,1,0:T(8,128)(2,1)S(1)}, u32[]{:S(2)}, u32[]{:S(2)}) async-start(bf16[64,8,128]{2,1,0:T(8,128)(2,1)} %bitcast.14), calls=%async_computation.1 | async-start | bytes 262144 | tf_op jit(solution)/shard_map/all_to_all | solution.py:28
  65.2 0.0 reduce-scatter.2.cloned.1.call-start
  65.2 0.1 iota_compare_fusion
  65.3 15.4 %all-to-all-done.1 = bf16[64,8,128]{2,1,0:T(8,128)(2,1)S(1)} async-done(((bf16[64,8,128]{2,1,0:T(8,128)(2,1)}), bf16[64,8,128]{2,1,0:T(8,128)(2,1)S(1)}, u32[]{:S(2)}, u32[]{:S(2)}) %all-to-all-start.1) | async-done | bytes 131104 | tf_op jit(solution)/shard_map/all_to_all | solution.py:28
  80.7 1.6 fusion.13
  82.3 2.7 %multiply_reduce_fusion = (f32[512,4]{0,1:T(4,128)S(1)}, f32[512,4,128]{0,2,1:T(8,128)S(1)}) fusion(f32[4,128,512]{2,1,0:T(8,128)} %fusion.13, bf16[512,4,128]{0,2,1:T(8,128)(2,1)S(1)} %bitcast.41, bf16[512,4,128]{0,2,1:T(8,128)(2,1)S(1)} %bitcast.39, pred[512,512]{1,0:T(8,128)(4,1)S(1)} %iota_compare_fusion, bf16[512,512]{1,0:T(8,128)(2,1)S(1)} %copy-done.3), kind=kOutput, calls=%fused_computation.18 | convolution fusion | flops 541325312 | bytes 3940352 | tf_op jit(solution)/shard_map/hts,she->the/dot_general | solution.py:75
  85.0 0.2 multiply_convert_fusion
  85.2 0.2 copy.19.normed_ref
  85.4 24.4 %all-gather.2.cloned.1.call-done = bf16[4096,512]{1,0:T(8,128)(2,1)} async-done(((bf16[256,512]{1,0:T(8,128)(2,1)}), bf16[4096,512]{1,0:T(8,128)(2,1)}) %all-gather.2.cloned.1.call-update) | async-done | bytes 4194320 | tf_op jit(solution)/shard_map/all_gather | solution.py:64
  109.8 2.2 %copy-done.1 = bf16[4096,512]{1,0:T(8,128)(2,1)S(1)} copy-done((bf16[4096,512]{1,0:T(8,128)(2,1)S(1)}, bf16[4096,512]{1,0:T(8,128)(2,1)}, u32[]{:S(2)}) %copy-start.1) | copy-done | bytes 4194328
  111.9 4.4 %shard_map.55 = bf16[512,4096]{1,0:T(8,128)(2,1)S(1)} custom-call(bf16[512,512]{1,0:T(8,128)(2,1)S(1)} %copy.19.normed_ref, bf16[16,4,64,512]{3,2,1,0:T(8,128)(2,1)S(1)} %bitcast.37), custom_call_target="tpu_custom_call" | custom-call | flops 2147483648 | bytes 9437184 | tf_op jit(solution)/shard_map/pallas_call | solution.py:43
  116.3 1.9 %copy-done = bf16[512,4096]{1,0:T(8,128)(2,1)} copy-done((bf16[512,4096]{1,0:T(8,128)(2,1)}, bf16[512,4096]{1,0:T(8,128)(2,1)S(1)}, u32[]{:S(2)}) %copy-start) | copy-done | bytes 4194328
  118.3 0.0 reduce-scatter.2.cloned.1.call-update
  118.3 42.2 %reduce-scatter.2.cloned.1.call-done = bf16[64,4096]{1,0:T(8,128)(2,1)} async-done(((bf16[512,4096]{1,0:T(8,128)(2,1)}), bf16[64,4096]{1,0:T(8,128)(2,1)}) %reduce-scatter.2.cloned.1.call-update) | async-done | bytes 524304 | tf_op jit(solution)/shard_map/reduce_scatter | solution.py:83
  (9 shorter events, 0.0 us)
Async XLA Ops:
  6.5 74.2 %copy-start.3 = (bf16[512,512]{1,0:T(8,128)(2,1)S(1)}, bf16[512,512]{1,0:T(8,128)(2,1)}, u32[]{:S(2)}) copy-start(bf16[512,512]{1,0:T(8,128)(2,1)} %param.5) | copy-start | bytes 1572868
  6.5 103.2 %all-gather.2.cloned.1.call-start = ((), (), s32[]{:S(2)}) async-start(), calls=%async_computation.3 | async-start | bytes 4456448 | tf_op jit(solution)/shard_map/all_gather | solution.py:64
  27.7 30.3 %all-to-all-start = ((bf16[64,8,128]{2,1,0:T(8,128)(2,1)}), bf16[64,8,128]{2,1,0:T(8,128)(2,1)S(1)}, u32[]{:S(2)}, u32[]{:S(2)}) async-start(bf16[64,8,128]{2,1,0:T(8,128)(2,1)} %bitcast.2), calls=%async_computation | async-start | bytes 262144 | tf_op jit(solution)/shard_map/all_to_all | solution.py:24
  58.9 21.8 %all-to-all-start.1 = ((bf16[64,8,128]{2,1,0:T(8,128)(2,1)}), bf16[64,8,128]{2,1,0:T(8,128)(2,1)S(1)}, u32[]{:S(2)}, u32[]{:S(2)}) async-start(bf16[64,8,128]{2,1,0:T(8,128)(2,1)} %bitcast.14), calls=%async_computation.1 | async-start | bytes 262144 | tf_op jit(solution)/shard_map/all_to_all | solution.py:28
  65.2 95.3 %reduce-scatter.2.cloned.1.call-start = ((), (), s32[]{:S(2)}) async-start(), calls=%async_computation.4 | async-start | bytes 4718592 | tf_op jit(solution)/shard_map/reduce_scatter | solution.py:83
  82.3 2.7 %copy-start.2 = (f32[512]{0:T(512)S(1)}, f32[512]{0:T(512)}, u32[]{:S(2)}) copy-start(f32[512]{0:T(512)} %param.9) | copy-start | bytes 6148
  109.8 2.2 %copy-start.1 = (bf16[4096,512]{1,0:T(8,128)(2,1)S(1)}, bf16[4096,512]{1,0:T(8,128)(2,1)}, u32[]{:S(2)}) copy-start(bf16[4096,512]{1,0:T(8,128)(2,1)} %all-gather.2.cloned.1.call-done) | copy-start | bytes 12582916
  116.3 1.9 %copy-start = (bf16[512,4096]{1,0:T(8,128)(2,1)}, bf16[512,4096]{1,0:T(8,128)(2,1)S(1)}, u32[]{:S(2)}) copy-start(bf16[512,4096]{1,0:T(8,128)(2,1)S(1)} %shard_map.55) | copy-start | bytes 12582916
Sparse Core Ops, SparseCore 0:
  23.8 85.8 all-gather.1
  118.4 42.0 reduce-scatter.1

commit v2 on v0

v2 whole, which is shorter than its diff:
```python
import jax
import jax.numpy as jnp
from jax import lax
from jax.experimental import pallas as pl
from jax.experimental.pallas import tpu as pltpu
from jax.sharding import PartitionSpec as P

DH = 128
NX, NY, NZ = 4, 4, 16
Z_GROUPS = [[y * NZ + z for z in range(NZ)] for y in range(NY)]
X_GROUPS = [[0, 2, 4, 6], [1, 3, 5, 7]]
CORES = [(i, i ^ 1) for i in range(8)]
VMEM = pl.BlockSpec(memory_space=pltpu.VMEM)
f32, bf16 = jnp.float32, jnp.bfloat16


def call(kernel, outs, flops, *args):
    return pl.pallas_call(
        kernel,
        in_specs=[VMEM] * len(args),
        out_specs=[VMEM] * len(outs),
        out_shape=outs,
        compiler_params=pltpu.CompilerParams(vmem_limit_bytes=16 << 20),
        cost_estimate=pl.CostEstimate(flops=flops, bytes_accessed=4 << 20, transcendentals=1 << 18),
    )(*args)


def placed_call(kernel, out, flops, place, *args):
    return pl.pallas_call(
        kernel,
        in_specs=[pl.BlockSpec(memory_space=pltpu.SMEM)] + [VMEM] * len(args),
        out_specs=VMEM,
        out_shape=out,
        compiler_params=pltpu.CompilerParams(vmem_limit_bytes=16 << 20),
        cost_estimate=pl.CostEstimate(flops=flops, bytes_accessed=4 << 20, transcendentals=0),
    )(place, *args)


def feature(x):
    x = x.astype(f32)
    return jnp.where(x > 0.0, x + 1.0, jnp.exp(jnp.minimum(x, 0.0))).astype(bf16)


def heads(ref):
    return [slice(h * DH, (h + 1) * DH) for h in range(ref.shape[1] // DH)]


def memory_kernel(keys_ref, values_ref, key_ref, memory_ref):
    for cols in heads(keys_ref):
        key = feature(keys_ref[:, cols])
        key_ref[:, cols] = key
        memory_ref[cols, :] = lax.dot_general(
            key, values_ref[:, cols], (((0,), (0,)), ((), ())), preferred_element_type=f32
        ).astype(bf16)


def local_kernel(queries_ref, key_ref, values_ref, query_ref, attended_ref):
    rows = queries_ref.shape[0]
    step = 256
    for cols in heads(queries_ref):
        query_ref[:, cols] = feature(queries_ref[:, cols])
        for top in range(0, rows, step):
            seen = top + step
            scores = lax.dot_general(
                query_ref[top:seen, cols],
                key_ref[:seen, cols],
                (((1,), (1,)), ((), ())),
                preferred_element_type=f32,
            )
            row = top + lax.broadcasted_iota(jnp.int32, scores.shape, 0)
            column = lax.broadcasted_iota(jnp.int32, scores.shape, 1)
            weights = jnp.where(column <= row, scores, 0.0).astype(bf16)
            attended_ref[top:seen, cols] = jnp.dot(
                weights, values_ref[:seen, cols], preferred_element_type=f32
            )


def prior_kernel(pieces_ref, sums_ref):
    total = jnp.zeros(pieces_ref.shape[1:], f32)
    for block in range(pieces_ref.shape[0]):
        sums_ref[block] = total.astype(bf16)
        total = total + pieces_ref[block].astype(f32)


def split_norm_kernel(core_ref, query_ref, prior_ref, attended_ref, gain_ref, normed_ref):
    core = core_ref[0]
    _, chips, rows, _ = normed_ref.shape
    for cols in heads(query_ref):
        attended = attended_ref[:, cols] + jnp.dot(
            query_ref[:, cols], prior_ref[cols, :], preferred_element_type=f32
        )
        mean_square = jnp.mean(attended * attended, axis=-1, keepdims=True)
        normed = (attended * lax.rsqrt(mean_square + 1e-05) * gain_ref[:, cols]).astype(bf16)
        for chip in range(chips):
            for side in range(2):
                top = (2 * chip + side) * rows
                normed_ref[(core + side) % 2, chip, :, cols] = normed[top : top + rows]


def product(y, tokens_ref, weight_ref, side):
    zs, chips, cols, depth = weight_ref.shape
    total = None
    for turn in range(chips):
        tokens = tokens_ref[(y + turn) % chips, side].reshape(-1, depth)
        weight = weight_ref[:, turn].reshape(zs * cols, depth)
        term = lax.dot_general(tokens, weight, (((1,), (1,)), ((), ())), preferred_element_type=f32)
        total = term if total is None else total + term
    return total


def theirs_kernel(place_ref, tokens_ref, weight_ref, out_ref):
    out_ref[...] = product(place_ref[0], tokens_ref, weight_ref, 1).astype(bf16)


def mine_kernel(place_ref, tokens_ref, weight_ref, got_ref, out_ref):
    total = product(place_ref[0], tokens_ref, weight_ref, 0)
    out_ref[...] = (total + got_ref[...].astype(f32)).astype(bf16)


def project(kernel, place, tokens, weight, *more):
    _, _, chips, rows, depth = tokens.shape
    zs, turns, cols, _ = weight.shape
    step = 4
    block = pl.BlockSpec((chips * rows, step * cols), lambda z: (0, z))
    return pl.pallas_call(
        kernel,
        grid=(zs // step,),
        in_specs=[
            pl.BlockSpec(memory_space=pltpu.SMEM),
            pl.BlockSpec(tokens.shape, lambda z: (0,) * tokens.ndim),
            pl.BlockSpec((step, turns, cols, depth), lambda z: (z, 0, 0, 0)),
            *[block for _ in more],
        ],
        out_specs=block,
        out_shape=jax.ShapeDtypeStruct((chips * rows, zs * cols), bf16),
        compiler_params=pltpu.CompilerParams(vmem_limit_bytes=48 << 20),
        cost_estimate=pl.CostEstimate(
            flops=2 * chips * rows * turns * depth * zs * cols, bytes_accessed=7 << 20, transcendentals=0
        ),
    )(place, tokens, weight, *more)


def join_kernel(parts_ref, out_ref):
    chips, _, cols = parts_ref.shape
    for chip in range(chips):
        out_ref[:, chip * cols : (chip + 1) * cols] = parts_ref[chip]


def to_plane(turn):
    pairs = []
    for y in range(NY):
        for z in range(NZ):
            for x in range(NX):
                for core in range(2):
                    source = (y * NZ + z) * 2 * NX + 2 * x + core
                    target = ((x - turn) % NY * NZ + z) * 2 * NX + 2 * y + core
                    pairs.append((source, target))
    return pairs


def body(queries, keys, values, out_weight, head_gain):
    rows, width = queries.shape
    shape = lambda dims, kind: jax.ShapeDtypeStruct(dims, kind)
    blocks = lax.axis_size("seq")
    y = (lax.axis_index("seq").astype(jnp.int32) // NZ).reshape(1)
    core = (lax.axis_index("head").astype(jnp.int32) % 2).reshape(1)

    own = out_weight.T
    planes = [lax.ppermute(own, ("seq", "head"), to_plane(turn)) for turn in range(NX)]
    weight = lax.all_gather(jnp.concatenate(planes), "seq", axis=0, tiled=True, axis_index_groups=Z_GROUPS)

    key, memory = call(memory_kernel, [shape((rows, width), bf16), shape((width, DH), bf16)], 1 << 26, keys, values)
    pieces = lax.all_to_all(memory.reshape(blocks, -1, DH), "seq", 0, 0, tiled=True)
    (sums,) = call(prior_kernel, [shape(pieces.shape, bf16)], 1 << 16, pieces)
    prior = lax.all_to_all(sums, "seq", 0, 0, tiled=True).reshape(width, DH)
    query, attended = call(
        local_kernel, [shape((rows, width), bf16), shape((rows, width), f32)], 1 << 28, queries, key, values
    )
    normed = placed_call(
        split_norm_kernel,
        shape((2, NX, rows // 8, width), bf16),
        1 << 26,
        core,
        query,
        prior,
        attended,
        head_gain.reshape(1, -1),
    )
    copies = jnp.broadcast_to(normed[None], (NX, *normed.shape))
    tokens = lax.all_to_all(copies, "head", 0, 0, tiled=True, axis_index_groups=X_GROUPS)

    weight = weight.reshape(NZ, NX, *own.shape)
    theirs = project(theirs_kernel, y, tokens, weight)
    got = lax.ppermute(theirs, "head", CORES)
    mine = project(mine_kernel, y, tokens, weight, got)
    parts = lax.all_to_all(mine.reshape(NX, rows // 8, -1), "head", 0, 0, tiled=True, axis_index_groups=X_GROUPS)
    (out,) = call(join_kernel, [shape((rows // 8, NX * parts.shape[-1]), bf16)], 1 << 16, parts)
    return out


def solution(mesh):
    placed = (P("seq", "head"), P("seq", "head"), P("seq", "head"), P("head", "seq"), P("head"))
    return jax.shard_map(
        body, mesh=mesh, in_specs=placed, out_specs=P(("seq", "head"), None), check_vma=False
    )
```

time: 410 us -> 153 us (0.37)
  waiting for transfers between devices: 312 us -> 46.1 us
  other arithmetic: 67.3 us -> 0.72 us
  blocking collectives: 0 us -> 48.9 us
  starting transfers between devices: 0.08 us -> 27.3 us
  matrix products: 12.2 us -> 0 us
  Pallas kernels: 0 us -> 12.1 us
    all_gather x2 -> x1, waiting for transfers between devices: 269 us -> 0.6 us  [body(): lax.all_gather(jnp.concatenate(planes), 'seq', axis=0, tiled=True, axis_i...]
    select_n x63 -> x0, other arithmetic: 65.6 us -> none  [lap(): return jnp.where(position < mine, longer, subtotal)]
    all_to_all x0 -> x2, blocking collectives: none -> 48.9 us  [the longest x1 34.9 us: body(): lax.all_to_all(memory.reshape(blocks, -1, DH), 'seq', 0, 0, tiled=True)]
    reduce_scatter x1 -> x0, waiting for transfers between devices: 42.4 us -> none  [body(): lax.psum_scatter(jnp.dot(normed, weight_rows, preferred_element_type=jnp....]
    all_to_all x0 -> x2, waiting for transfers between devices: none -> 38.3 us  [the longest x1 23.9 us: body(): lax.all_to_all(copies, 'head', 0, 0, tiled=True, axis_index_groups=X_GROUPS)]
    ppermute x0 -> x5, starting transfers between devices: none -> 16.9 us  [the longest x4 15 us: body(): lax.ppermute(own, ('seq', 'head'), to_plane(turn))]
    dot_general x4 -> x0, matrix products: 12.2 us -> none  [the longest x1 6.53 us: body(): jnp.dot(normed, weight_rows, preferred_element_type=jnp.float32)]
    pallas_call x0 -> x7, Pallas kernels: none -> 12.1 us  [the longest x2 8.01 us: project(): pl.pallas_call(kernel, grid=(zs // step,), in_specs=[pl.BlockSpec(memory_...]
  transfers between devices with their start and end apart: 3 -> 8, of which waited for: 3 -> 5; matrix products, arithmetic and copies ran while one was open for 17% -> 1% of each run, Pallas kernels for 0% -> 2%
where the time goes in v2:
time: 153 us; the launch traced here: 152 us
  blocking collectives  48.9 us (32%)
  waiting for transfers between devices  46.1 us (30%)
  starting transfers between devices  27.3 us (18%)
  between operations  13.5 us (9%)
  Pallas kernels  12.1 us (8%)
  local copies, waits for them, and re-layouts  3.69 us (2%)
    all_to_all x1, blocking collectives, body(): lax.all_to_all(memory.reshape(blocks, -1, DH), 'seq', 0, 0, tiled=True)  34.9 us
    all_to_all x1, waiting for transfers between devices, body(): lax.all_to_all(copies, 'head', 0, 0, tiled=True, axis_index_groups=X_GROUPS)  23.9 us
    ppermute x4, starting transfers between devices, body(): lax.ppermute(own, ('seq', 'head'), to_plane(turn))  15 us
    all_to_all x1, waiting for transfers between devices, body(): prior = lax.all_to_all(sums, 'seq', 0, 0, tiled=True).reshape(width, DH)  14.4 us
    all_to_all x1, blocking collectives, body(): lax.all_to_all(mine.reshape(NX, rows // 8, -1), 'head', 0, 0, tiled=True,...  14 us
    pallas_call x2, Pallas kernels, project(): pl.pallas_call(kernel, grid=(zs // step,), in_specs=[pl.BlockSpec(memory_...  8.01 us
    all_to_all x1, starting transfers between devices, body(): prior = lax.all_to_all(sums, 'seq', 0, 0, tiled=True).reshape(width, DH)  6.28 us
    ppermute x4, waiting for transfers between devices, body(): lax.ppermute(own, ('seq', 'head'), to_plane(turn))  5.3 us
  transfers between devices with their start and end apart: 8, of which 5 were waited for; matrix products, arithmetic and copies ran while one was open for 1% of the time, Pallas kernels for 2%

profile of v2, /device:TPU:24, one launch (start us, length us, event | category | flops | bytes accessed | tf_op | source)
XLA Modules:
  0.0 152.3 jit_solution(1361275340229180163)
XLA Ops:
  6.5 4.4 %collective-permute-start = (bf16[64,512]{1,0:T(8,128)(2,1)}, bf16[64,512]{1,0:T(8,128)(2,1)S(1)}, u32[]{:S(2)}, u32[]{:S(2)}) collective-permute-start(bf16[64,512]{1,0:T(8,128)(2,1)} %bitcast.14), channel_id=1, source_target_pairs={{0,0},{1,1},{2,128},{3,129},{4,256},{5,257},{6,384},{7,385},{8,8},... | collective-permute-start | bytes 196616 | tf_op jit(solution)/shard_map/ppermute | solution.py:169
  11.0 1.9 %collective-permute-start.1 = (bf16[64,512]{1,0:T(8,128)(2,1)}, bf16[64,512]{1,0:T(8,128)(2,1)S(1)}, u32[]{:S(2)}, u32[]{:S(2)}) collective-permute-start(bf16[64,512]{1,0:T(8,128)(2,1)} %bitcast.15), channel_id=1, source_target_pairs={{0,384},{1,385},{2,0},{3,1},{4,128},{5,129},{6,256},{7,257},{8,392... | collective-permute-start | bytes 196616 | tf_op jit(solution)/shard_map/ppermute | solution.py:169
  12.9 4.0 %collective-permute-start.2 = (bf16[64,512]{1,0:T(8,128)(2,1)}, bf16[64,512]{1,0:T(8,128)(2,1)S(1)}, u32[]{:S(2)}, u32[]{:S(2)}) collective-permute-start(bf16[64,512]{1,0:T(8,128)(2,1)} %bitcast.16), channel_id=1, source_target_pairs={{0,256},{1,257},{2,384},{3,385},{4,0},{5,1},{6,128},{7,129},{8,264... | collective-permute-start | bytes 196616 | tf_op jit(solution)/shard_map/ppermute | solution.py:169
  16.9 4.6 %collective-permute-start.3 = (bf16[64,512]{1,0:T(8,128)(2,1)}, bf16[64,512]{1,0:T(8,128)(2,1)S(1)}, u32[]{:S(2)}, u32[]{:S(2)}) collective-permute-start(bf16[64,512]{1,0:T(8,128)(2,1)} %bitcast.17), channel_id=1, source_target_pairs={{0,128},{1,129},{2,256},{3,257},{4,384},{5,385},{6,0},{7,1},{8,136... | collective-permute-start | bytes 196616 | tf_op jit(solution)/shard_map/ppermute | solution.py:169
  21.6 5.3 %collective-permute-done.3 = bf16[64,512]{1,0:T(8,128)(2,1)S(1)} collective-permute-done((bf16[64,512]{1,0:T(8,128)(2,1)}, bf16[64,512]{1,0:T(8,128)(2,1)S(1)}, u32[]{:S(2)}, u32[]{:S(2)}) %collective-permute-start.3) | collective-permute-done | bytes 65568 | tf_op jit(solution)/shard_map/ppermute | solution.py:169
  26.9 0.7 pad_maximum_fusion
  27.6 1.0 copy-done
  28.7 1.0 copy-done.3
  29.7 0.5 shard_map.55
  30.3 34.9 %all_to_all.20.pieces_ref = bf16[64,8,128]{2,1,0:T(8,128)(2,1)S(1)} all-to-all(bf16[64,8,128]{2,1,0:T(8,128)(2,1)S(1)} %bitcast.10), channel_id=1, replica_groups=mesh['seq'=64,'head'=8] {'seq'}, dimensions={0} | all-to-all | bytes 262144 | tf_op jit(solution)/shard_map/all_to_all | solution.py:173
  65.1 0.7 shard_map.57
  65.9 6.3 %all-to-all-start.1 = ((bf16[64,8,128]{2,1,0:T(8,128)(2,1)}), bf16[64,8,128]{2,1,0:T(8,128)(2,1)S(1)}, u32[]{:S(2)}, u32[]{:S(2)}) async-start(bf16[64,8,128]{2,1,0:T(8,128)(2,1)} %shard_map.57), calls=%async_computation.1 | async-start | bytes 262144 | tf_op jit(solution)/shard_map/all_to_all | solution.py:175
  72.2 1.5 shard_map.56
  73.7 14.4 %all-to-all-done.1 = bf16[64,8,128]{2,1,0:T(8,128)(2,1)S(1)} async-done(((bf16[64,8,128]{2,1,0:T(8,128)(2,1)}), bf16[64,8,128]{2,1,0:T(8,128)(2,1)S(1)}, u32[]{:S(2)}, u32[]{:S(2)}) %all-to-all-start.1) | async-done | bytes 131104 | tf_op jit(solution)/shard_map/all_to_all | solution.py:175
  88.6 1.6 %broadcast_in_dim.2 = bf16[4,2,4,64,512]{4,3,2,1,0:T(8,128)(2,1)} broadcast(bf16[2,4,64,512]{3,2,1,0:T(8,128)(2,1)S(1)} %shard_map.58), dimensions={1,2,3,4} | broadcast | bytes 2621440 | tf_op jit(solution)/shard_map/broadcast_in_dim | solution.py:189
  90.2 4.1 %all-to-all-start.2 = ((bf16[4,2,4,64,512]{4,3,2,1,0:T(8,128)(2,1)}), bf16[4,2,4,64,512]{4,3,2,1,0:T(8,128)(2,1)S(1)}, u32[]{:S(2)}, u32[]{:S(2)}) async-start(bf16[4,2,4,64,512]{4,3,2,1,0:T(8,128)(2,1)} %broadcast_in_dim.2), calls=%async_computation.2 | async-start | bytes 4194304 | tf_op jit(solution)/shard_map/all_to_all | solution.py:190
  94.3 23.9 %all-to-all-done.2.tokens_ref = bf16[4,2,4,64,512]{4,3,2,1,0:T(8,128)(2,1)S(1)} async-done(((bf16[4,2,4,64,512]{4,3,2,1,0:T(8,128)(2,1)}), bf16[4,2,4,64,512]{4,3,2,1,0:T(8,128)(2,1)S(1)}, u32[]{:S(2)}, u32[]{:S(2)}) %all-to-all-start.2) | async-done | bytes 2097184 | tf_op jit(solution)/shard_map/all_to_all | solution.py:190
  118.2 0.6 all-gather.2.cloned.1.call-done
  118.8 4.0 %shard_map.59 = bf16[256,1024]{1,0:T(8,128)(2,1)S(1)} custom-call(s32[1]{0:T(128)} %bitcast.place_ref, bf16[4,2,4,64,512]{4,3,2,1,0:T(8,128)(2,1)S(1)} %all-to-all-done.2.tokens_ref, bf16[16,4,64,512]{3,2,1,0:T(8,128)(2,1)} %bitcast.12), custom_call_target="tpu_custom_call" | custom-call | flops 1073741824 | bytes 7340032 | tf_op jit(solution)/shard_map/pallas_call | solution.py:125
  122.8 1.9 %collective-permute-start.4 = (bf16[256,1024]{1,0:T(8,128)(2,1)S(1)}, bf16[256,1024]{1,0:T(8,128)(2,1)S(1)}, u32[]{:S(2)}, u32[]{:S(2)}) collective-permute-start(bf16[256,1024]{1,0:T(8,128)(2,1)S(1)} %shard_map.59), channel_id=1, source_target_pairs={{0,1},{1,0},{2,3},{3,2},{4,5},{5,4},{6,7},{7,6},{8,9},{9,8},{10,11... | collective-permute-start | bytes 1572872 | tf_op jit(solution)/shard_map/ppermute | solution.py:194
  124.8 1.9 %collective-permute-done.4.got_ref = bf16[256,1024]{1,0:T(8,128)(2,1)S(1)} collective-permute-done((bf16[256,1024]{1,0:T(8,128)(2,1)S(1)}, bf16[256,1024]{1,0:T(8,128)(2,1)S(1)}, u32[]{:S(2)}, u32[]{:S(2)}) %collective-permute-start.4) | collective-permute-done | bytes 524320 | tf_op jit(solution)/shard_map/ppermute | solution.py:194
  126.6 4.0 %shard_map.60 = bf16[256,1024]{1,0:T(8,128)(2,1)S(1)} custom-call(s32[1]{0:T(128)} %bitcast.place_ref, bf16[4,2,4,64,512]{4,3,2,1,0:T(8,128)(2,1)S(1)} %all-to-all-done.2.tokens_ref, bf16[16,4,64,512]{3,2,1,0:T(8,128)(2,1)} %bitcast.13, bf16[256,1024]{1,0:T(8,128)(2,1)S(1)} %collective-permute-done.4.got_ref), custom_call_target="tpu_custom_call" | custom-call | flops 1073741824 | bytes 7340032 | tf_op jit(solution)/shard_map/pallas_call | solution.py:125
  130.7 14.0 %all_to_all.21.parts_ref = bf16[4,64,1024]{2,1,0:T(8,128)(2,1)S(1)} all-to-all(bf16[4,64,1024]{2,1,0:T(8,128)(2,1)S(1)} %bitcast.8), channel_id=1, replica_groups={{0,2,4,6},{1,3,5,7},{8,10,12,14},{9,11,13,15},{16,18,20,22},{17,19,21,2..., dimensions={0} | all-to-all | bytes 1048576 | tf_op jit(solution)/shard_map/all_to_all | solution.py:196
  144.7 0.8 shard_map.61
  (14 shorter events, 0.6 us)
Async XLA Ops:
  6.5 65.6 %copy-start.1 = (bf16[512,512]{1,0:T(8,128)(2,1)S(1)}, bf16[512,512]{1,0:T(8,128)(2,1)}, u32[]{:S(2)}) copy-start(bf16[512,512]{1,0:T(8,128)(2,1)} %values_ref.3) | copy-start | bytes 1572868
  6.5 112.3 %all-gather.2.cloned.1.call-start = ((), (), s32[]{:S(2)}) async-start(), calls=%async_computation.4 | async-start | bytes 4456448 | tf_op jit(solution)/shard_map/all_gather | solution.py:170
  6.5 15.0 %collective-permute-start = (bf16[64,512]{1,0:T(8,128)(2,1)}, bf16[64,512]{1,0:T(8,128)(2,1)S(1)}, u32[]{:S(2)}, u32[]{:S(2)}) collective-permute-start(bf16[64,512]{1,0:T(8,128)(2,1)} %bitcast.14), channel_id=1, source_target_pairs={{0,0},{1,1},{2,128},{3,129},{4,256},{5,257},{6,384},{7,385},{8,8},... | collective-permute-start | bytes 196616 | tf_op jit(solution)/shard_map/ppermute | solution.py:169
  11.0 10.6 %collective-permute-start.1 = (bf16[64,512]{1,0:T(8,128)(2,1)}, bf16[64,512]{1,0:T(8,128)(2,1)S(1)}, u32[]{:S(2)}, u32[]{:S(2)}) collective-permute-start(bf16[64,512]{1,0:T(8,128)(2,1)} %bitcast.15), channel_id=1, source_target_pairs={{0,384},{1,385},{2,0},{3,1},{4,128},{5,129},{6,256},{7,257},{8,392... | collective-permute-start | bytes 196616 | tf_op jit(solution)/shard_map/ppermute | solution.py:169
  12.9 8.7 %collective-permute-start.2 = (bf16[64,512]{1,0:T(8,128)(2,1)}, bf16[64,512]{1,0:T(8,128)(2,1)S(1)}, u32[]{:S(2)}, u32[]{:S(2)}) collective-permute-start(bf16[64,512]{1,0:T(8,128)(2,1)} %bitcast.16), channel_id=1, source_target_pairs={{0,256},{1,257},{2,384},{3,385},{4,0},{5,1},{6,128},{7,129},{8,264... | collective-permute-start | bytes 196616 | tf_op jit(solution)/shard_map/ppermute | solution.py:169
  16.9 10.0 %collective-permute-start.3 = (bf16[64,512]{1,0:T(8,128)(2,1)}, bf16[64,512]{1,0:T(8,128)(2,1)S(1)}, u32[]{:S(2)}, u32[]{:S(2)}) collective-permute-start(bf16[64,512]{1,0:T(8,128)(2,1)} %bitcast.17), channel_id=1, source_target_pairs={{0,128},{1,129},{2,256},{3,257},{4,384},{5,385},{6,0},{7,1},{8,136... | collective-permute-start | bytes 196616 | tf_op jit(solution)/shard_map/ppermute | solution.py:169
  27.6 60.4 %copy-start.4 = (f32[512]{0:T(512)S(1)}, f32[512]{0:T(512)}, u32[]{:S(2)}) copy-start(f32[512]{0:T(512)} %param.9) | copy-start | bytes 6148
  27.6 1.0 copy-start
  28.7 1.0 copy-start.3
  29.7 42.5 %copy-start.2 = (bf16[512,512]{1,0:T(8,128)(2,1)S(1)}, bf16[512,512]{1,0:T(8,128)(2,1)}, u32[]{:S(2)}) copy-start(bf16[512,512]{1,0:T(8,128)(2,1)} %queries_ref.1) | copy-start | bytes 1572868
  65.9 22.2 %all-to-all-start.1 = ((bf16[64,8,128]{2,1,0:T(8,128)(2,1)}), bf16[64,8,128]{2,1,0:T(8,128)(2,1)S(1)}, u32[]{:S(2)}, u32[]{:S(2)}) async-start(bf16[64,8,128]{2,1,0:T(8,128)(2,1)} %shard_map.57), calls=%async_computation.1 | async-start | bytes 262144 | tf_op jit(solution)/shard_map/all_to_all | solution.py:175
  90.2 28.0 %all-to-all-start.2 = ((bf16[4,2,4,64,512]{4,3,2,1,0:T(8,128)(2,1)}), bf16[4,2,4,64,512]{4,3,2,1,0:T(8,128)(2,1)S(1)}, u32[]{:S(2)}, u32[]{:S(2)}) async-start(bf16[4,2,4,64,512]{4,3,2,1,0:T(8,128)(2,1)} %broadcast_in_dim.2), calls=%async_computation.2 | async-start | bytes 4194304 | tf_op jit(solution)/shard_map/all_to_all | solution.py:190
  122.8 3.8 %collective-permute-start.4 = (bf16[256,1024]{1,0:T(8,128)(2,1)S(1)}, bf16[256,1024]{1,0:T(8,128)(2,1)S(1)}, u32[]{:S(2)}, u32[]{:S(2)}) collective-permute-start(bf16[256,1024]{1,0:T(8,128)(2,1)S(1)} %shard_map.59), channel_id=1, source_target_pairs={{0,1},{1,0},{2,3},{3,2},{4,5},{5,4},{6,7},{7,6},{8,9},{9,8},{10,11... | collective-permute-start | bytes 1572872 | tf_op jit(solution)/shard_map/ppermute | solution.py:194
Sparse Core Ops, SparseCore 0:
  27.8 91.0 all-gather.1

commit v3 on v2

--- a/solution.py
+++ b/solution.py
@@ -7,7 +7,7 @@
 
 DH = 128
 NX, NY, NZ = 4, 4, 16
-Z_GROUPS = [[y * NZ + z for z in range(NZ)] for y in range(NY)]
+NL = 4
 X_GROUPS = [[0, 2, 4, 6], [1, 3, 5, 7]]
 CORES = [(i, i ^ 1) for i in range(8)]
 VMEM = pl.BlockSpec(memory_space=pltpu.VMEM)
@@ -29,7 +29,7 @@
     return pl.pallas_call(
         kernel,
         in_specs=[pl.BlockSpec(memory_space=pltpu.SMEM)] + [VMEM] * len(args),
-        out_specs=VMEM,
+        out_specs=jax.tree.map(lambda _: VMEM, out),
         out_shape=out,
         compiler_params=pltpu.CompilerParams(vmem_limit_bytes=16 << 20),
         cost_estimate=pl.CostEstimate(flops=flops, bytes_accessed=4 << 20, transcendentals=0),
@@ -97,47 +97,84 @@
                 normed_ref[(core + side) % 2, chip, :, cols] = normed[top : top + rows]
 
 
-def product(y, tokens_ref, weight_ref, side):
-    zs, chips, cols, depth = weight_ref.shape
-    total = None
-    for turn in range(chips):
-        tokens = tokens_ref[(y + turn) % chips, side].reshape(-1, depth)
-        weight = weight_ref[:, turn].reshape(zs * cols, depth)
-        term = lax.dot_general(tokens, weight, (((1,), (1,)), ((), ())), preferred_element_type=f32)
-        total = term if total is None else total + term
-    return total
-
-
-def theirs_kernel(place_ref, tokens_ref, weight_ref, out_ref):
-    out_ref[...] = product(place_ref[0], tokens_ref, weight_ref, 1).astype(bf16)
-
-
-def mine_kernel(place_ref, tokens_ref, weight_ref, got_ref, out_ref):
-    total = product(place_ref[0], tokens_ref, weight_ref, 0)
-    out_ref[...] = (total + got_ref[...].astype(f32)).astype(bf16)
-
-
-def project(kernel, place, tokens, weight, *more):
-    _, _, chips, rows, depth = tokens.shape
-    zs, turns, cols, _ = weight.shape
-    step = 4
-    block = pl.BlockSpec((chips * rows, step * cols), lambda z: (0, z))
+def stack_kernel(*refs):
+    *block_refs, stack_ref = refs
+    for index, block_ref in enumerate(block_refs):
+        stack_ref[index] = block_ref[...]
+
+
+def pass_kernel(block_ref, out_ref):
+    out_ref[...] = block_ref[...]
+
+
+def place_kernel(place_ref, *refs):
+    *stacks, low_ref, high_ref, arrived = refs
+    z = place_ref[0]
+    even = 1 - 2 * (z % 2)
+    half = NZ // 2
+    waits = []
+    for stack, shift in zip(stacks, (0, 1, -1, 2 * even)):
+        for index, turn in enumerate((0, 1, -1, 2)):
+            owner = (z - shift - NL * turn + 2 * NZ) % NZ
+            semaphore = arrived.at[len(waits)]
+            to_low = pltpu.make_async_copy(stack.at[index], low_ref.at[owner % half], semaphore)
+            to_high = pltpu.make_async_copy(stack.at[index], high_ref.at[owner % half], semaphore)
+            pl.when(owner < half)(to_low.start)
+            pl.when(owner >= half)(to_high.start)
+            waits.append(to_low)
+    for copy in waits:
+        copy.wait()
+
+
+def placed(z, stacks, cost):
+    half = jax.ShapeDtypeStruct((NZ // 2, *stacks[0].shape[1:]), bf16)
     return pl.pallas_call(
-        kernel,
-        grid=(zs // step,),
-        in_specs=[
-            pl.BlockSpec(memory_space=pltpu.SMEM),
-            pl.BlockSpec(tokens.shape, lambda z: (0,) * tokens.ndim),
-            pl.BlockSpec((step, turns, cols, depth), lambda z: (z, 0, 0, 0)),
-            *[block for _ in more],
-        ],
-        out_specs=block,
-        out_shape=jax.ShapeDtypeStruct((chips * rows, zs * cols), bf16),
-        compiler_params=pltpu.CompilerParams(vmem_limit_bytes=48 << 20),
-        cost_estimate=pl.CostEstimate(
-            flops=2 * chips * rows * turns * depth * zs * cols, bytes_accessed=7 << 20, transcendentals=0
-        ),
-    )(place, tokens, weight, *more)
+        place_kernel,
+        in_specs=[pl.BlockSpec(memory_space=pltpu.SMEM)] + [pl.BlockSpec(memory_space=pl.ANY)] * len(stacks),
+        out_specs=[VMEM, VMEM],
+        out_shape=[half, half],
+        scratch_shapes=[pltpu.SemaphoreType.DMA((NZ,))],
+        compiler_params=pltpu.CompilerParams(vmem_limit_bytes=56 << 20),
+        cost_estimate=pl.CostEstimate(flops=cost, bytes_accessed=2 << 20, transcendentals=0),
+    )(z, *stacks)
+
+
+def columns_of(weights, step=4):
+    at = 0
+    for weight in weights:
+        blocks, cols, depth = weight.shape
+        for first in range(0, blocks, step):
+            yield weight[first : first + step].reshape(step * cols, depth), slice(at, at + step * cols)
+            at += step * cols
+
+
+def times(tokens, weight):
+    return lax.dot_general(tokens, weight, (((1,), (1,)), ((), ())), preferred_element_type=f32)
+
+
+def features(tokens_ref, chip):
+    return tokens_ref[chip % NX].reshape(-1, tokens_ref.shape[-1])
+
+
+def near_kernel(place_ref, tokens_ref, *refs):
+    *halves, total_ref = refs
+    y = place_ref[0]
+    sources = [features(tokens_ref, y + turn) for turn in (0, NY - 1, 1)]
+    for terms in zip(*(columns_of(pair) for pair in zip(halves[::2], halves[1::2]))):
+        total_ref[:, terms[0][1]] = sum(times(tokens, weight) for tokens, (weight, _) in zip(sources, terms))
+
+
+def far_kernel(place_ref, tokens_ref, total_ref, first_ref, second_ref, mine_ref, theirs_ref):
+    tokens = features(tokens_ref, place_ref[0] + 2)
+    half = mine_ref.shape[0]
+    for weight, cols in columns_of([first_ref, second_ref]):
+        total = total_ref[:, cols] + times(tokens, weight)
+        mine_ref[:, cols] = total[:half]
+        theirs_ref[:, cols] = total[half:].astype(bf16)
+
+
+def add_kernel(mine_ref, got_ref, out_ref):
+    out_ref[...] = (mine_ref[...] + got_ref[...].astype(f32)).astype(bf16)
 
 
 def join_kernel(parts_ref, out_ref):
@@ -146,40 +183,61 @@
         out_ref[:, chip * cols : (chip + 1) * cols] = parts_ref[chip]
 
 
-def to_plane(turn):
+def to_plane(block):
     pairs = []
     for y in range(NY):
         for z in range(NZ):
             for x in range(NX):
                 for core in range(2):
                     source = (y * NZ + z) * 2 * NX + 2 * x + core
-                    target = ((x - turn) % NY * NZ + z) * 2 * NX + 2 * y + core
+                    target = (x * NZ + z) * 2 * NX + 2 * y + core
                     pairs.append((source, target))
-    return pairs
+    return lax.ppermute(block, ("seq", "head"), pairs)
+
+
+def along_z(block, shift):
+    pairs = [(y * NZ + z, y * NZ + (z + shift(z)) % NZ) for y in range(NY) for z in range(NZ)]
+    return lax.ppermute(block, "seq", pairs)
+
+
+def along_y(block, shift):
+    pairs = [(y * NZ + z, (y + shift) % NY * NZ + z) for y in range(NY) for z in range(NZ)]
+    return lax.ppermute(block, "seq", pairs)
+
+
+def after(value, *others):
+    return lax.optimization_barrier((value, *others))[0]
 
 
 def body(queries, keys, values, out_weight, head_gain):
     rows, width = queries.shape
     shape = lambda dims, kind: jax.ShapeDtypeStruct(dims, kind)
     blocks = lax.axis_size("seq")
-    y = (lax.axis_index("seq").astype(jnp.int32) // NZ).reshape(1)
+    place = lax.axis_index("seq").astype(jnp.int32)
+    y, z = (place // NZ).reshape(1), (place % NZ).reshape(1)
     core = (lax.axis_index("head").astype(jnp.int32) % 2).reshape(1)
 
-    own = out_weight.T
-    planes = [lax.ppermute(own, ("seq", "head"), to_plane(turn)) for turn in range(NX)]
-    weight = lax.all_gather(jnp.concatenate(planes), "seq", axis=0, tiled=True, axis_index_groups=Z_GROUPS)
-
+    own = to_plane(out_weight.T)
+    (own,) = call(pass_kernel, [shape(own.shape, bf16)], 1<<33, own)
+    far = [along_z(own, lambda z, s=s: s) for s in (NL, -NL, 2 * NL)]
     key, memory = call(memory_kernel, [shape((rows, width), bf16), shape((width, DH), bf16)], 1 << 26, keys, values)
     pieces = lax.all_to_all(memory.reshape(blocks, -1, DH), "seq", 0, 0, tiled=True)
-    (sums,) = call(prior_kernel, [shape(pieces.shape, bf16)], 1 << 16, pieces)
+    (stack,) = call(stack_kernel, [shape((NL, *own.shape), bf16)], 1<<33, own, *far)
+    near = [along_z(stack, s) for s in (lambda z: 1, lambda z: -1, lambda z: 2 - 4 * (z % 2))]
+    (sums,) = call(prior_kernel, [shape(pieces.shape, bf16)], 1<<33, pieces)
     prior = lax.all_to_all(sums, "seq", 0, 0, tiled=True).reshape(width, DH)
+    queries = after(queries, prior)
     query, attended = call(
         local_kernel, [shape((rows, width), bf16), shape((rows, width), f32)], 1 << 28, queries, key, values
     )
+    low, high = placed(z, [stack, *near], 1 << 33)
+    ahead_low, behind_high = along_y(low, 1), along_y(high, -1)
+    ahead_high, behind_low = along_y(high, 1), along_y(low, -1)
+    across = [along_y(ahead_low, 1), along_y(behind_high, -1)]
     normed = placed_call(
         split_norm_kernel,
         shape((2, NX, rows // 8, width), bf16),
-        1 << 26,
+        1<<33,
         core,
         query,
         prior,
@@ -189,12 +247,22 @@
     copies = jnp.broadcast_to(normed[None], (NX, *normed.shape))
     tokens = lax.all_to_all(copies, "head", 0, 0, tiled=True, axis_index_groups=X_GROUPS)
 
-    weight = weight.reshape(NZ, NX, *own.shape)
-    theirs = project(theirs_kernel, y, tokens, weight)
+    columns = NZ * own.shape[0]
+    halves = (low, high, ahead_low, ahead_high, behind_low, behind_high)
+    total = placed_call(near_kernel, shape((rows, columns), f32), 3 << 29, y, tokens, *halves)
+    mine, theirs = placed_call(
+        far_kernel,
+        [shape((rows // 2, columns), f32), shape((rows // 2, columns), bf16)],
+        1 << 29,
+        y,
+        tokens,
+        total,
+        *across,
+    )
     got = lax.ppermute(theirs, "head", CORES)
-    mine = project(mine_kernel, y, tokens, weight, got)
-    parts = lax.all_to_all(mine.reshape(NX, rows // 8, -1), "head", 0, 0, tiled=True, axis_index_groups=X_GROUPS)
-    (out,) = call(join_kernel, [shape((rows // 8, NX * parts.shape[-1]), bf16)], 1 << 16, parts)
+    (summed,) = call(add_kernel, [shape(theirs.shape, bf16)], 1 << 16, mine, got)
+    parts = lax.all_to_all(summed.reshape(NX, rows // 8, -1), "head", 0, 0, tiled=True, axis_index_groups=X_GROUPS)
+    (out,) = call(join_kernel, [shape((rows // 8, NX * columns), bf16)], 1 << 16, parts)
     return out
 
 

time: 153 us -> 141 us (0.922)
  starting transfers between devices: 27.3 us -> 85.5 us
  blocking collectives: 48.9 us -> 13.4 us
  waiting for transfers between devices: 46.1 us -> 21.9 us
  between operations: 13.5 us -> 0.39 us
  local copies, waits for them, and re-layouts: 3.69 us -> 6.62 us
    ppermute x4 -> x13, starting transfers between devices: 15 us -> 55.3 us  [the longest x6 32.1 us: along_z(): return lax.ppermute(block, 'seq', pairs)]
    all_to_all x2 -> x1, blocking collectives: 48.9 us -> 13.4 us  [body(): lax.all_to_all(summed.reshape(NX, rows // 8, -1), 'head', 0, 0, tiled=Tru...]
    all_to_all x1, waiting for transfers between devices: 23.9 us -> 0.01 us  [body(): lax.all_to_all(copies, 'head', 0, 0, tiled=True, axis_index_groups=X_GROUPS)]
    all_to_all x0 -> x1, starting transfers between devices: none -> 19.1 us  [body(): lax.all_to_all(memory.reshape(blocks, -1, DH), 'seq', 0, 0, tiled=True)]
    ppermute x4 -> x13, waiting for transfers between devices: 5.3 us -> 15.4 us  [the longest x6 15.4 us: along_y(): return lax.ppermute(block, 'seq', pairs)]
    all_to_all x1, waiting for transfers between devices: 14.4 us -> 4.67 us  [body(): prior = lax.all_to_all(sums, 'seq', 0, 0, tiled=True).reshape(width, DH)]
    pallas_call x2 -> x1, Pallas kernels: 8.01 us -> 2.35 us  [placed(): pl.pallas_call(place_kernel, in_specs=[pl.BlockSpec(memory_space=pltpu.SM...]
    pallas_call x1 -> x3, Pallas kernels: 0.51 us -> 5.46 us  [placed_call(): pl.pallas_call(kernel, in_specs=[pl.BlockSpec(memory_space=pltpu.SMEM)] +...]
  transfers between devices with their start and end apart: 8 -> 17, of which waited for: 5 -> 6; matrix products, arithmetic and copies ran while one was open for 1% -> 1% of each run, Pallas kernels for 2% -> 7%
where the time goes in v3:
time: 141 us; the launch traced here: 140 us
  starting transfers between devices  85.5 us (61%)
  waiting for transfers between devices  21.9 us (16%)
  blocking collectives  13.4 us (10%)
  Pallas kernels  12.1 us (9%)
  local copies, waits for them, and re-layouts  6.62 us (5%)
    ppermute x6, starting transfers between devices, along_z(): return lax.ppermute(block, 'seq', pairs)  32.1 us
    all_to_all x1, starting transfers between devices, body(): lax.all_to_all(memory.reshape(blocks, -1, DH), 'seq', 0, 0, tiled=True)  19.1 us
    ppermute x6, starting transfers between devices, along_y(): return lax.ppermute(block, 'seq', pairs)  18.9 us
    ppermute x6, waiting for transfers between devices, along_y(): return lax.ppermute(block, 'seq', pairs)  15.4 us
    all_to_all x1, blocking collectives, body(): lax.all_to_all(summed.reshape(NX, rows // 8, -1), 'head', 0, 0, tiled=Tru...  13.4 us
    all_to_all x1, starting transfers between devices, body(): prior = lax.all_to_all(sums, 'seq', 0, 0, tiled=True).reshape(width, DH)  5.51 us
    pallas_call x3, Pallas kernels, placed_call(): pl.pallas_call(kernel, in_specs=[pl.BlockSpec(memory_space=pltpu.SMEM)] +...  5.46 us
    unnamed x22, local copies, waits for them, and re-layouts  5.03 us
  transfers between devices with their start and end apart: 17, of which 6 were waited for; matrix products, arithmetic and copies ran while one was open for 1% of the time, Pallas kernels for 7%

profile of v3, /device:TPU:24, one launch (start us, length us, event | category | flops | bytes accessed | tf_op | source)
XLA Modules:
  0.0 139.9 jit_solution(3227171612557673130)
XLA Ops:
  0.0 4.3 %collective-permute-start = (bf16[64,512]{1,0:T(8,128)(2,1)}, bf16[64,512]{1,0:T(8,128)(2,1)S(1)}, u32[]{:S(2)}, u32[]{:S(2)}) collective-permute-start(bf16[64,512]{1,0:T(8,128)(2,1)} %bitcast.11), channel_id=1, source_target_pairs={{0,0},{1,1},{2,128},{3,129},{4,256},{5,257},{6,384},{7,385},{8,8},... | collective-permute-start | bytes 196616 | tf_op jit(solution)/shard_map/ppermute | solution.py:195
  7.6 19.1 %all-to-all-start = ((bf16[64,8,128]{2,1,0:T(8,128)(2,1)}), bf16[64,8,128]{2,1,0:T(8,128)(2,1)S(1)}, u32[]{:S(2)}, u32[]{:S(2)}) async-start(bf16[64,8,128]{2,1,0:T(8,128)(2,1)} %bitcast.2), calls=%async_computation | async-start | bytes 262144 | tf_op jit(solution)/shard_map/all_to_all | solution.py:224
  26.8 7.3 %collective-permute-start.1 = (bf16[64,512]{1,0:T(8,128)(2,1)S(1)}, bf16[64,512]{1,0:T(8,128)(2,1)S(1)}, u32[]{:S(2)}, u32[]{:S(2)}) collective-permute-start(bf16[64,512]{1,0:T(8,128)(2,1)S(1)} %shard_map.59.refs_0_), channel_id=1, source_target_pairs={{0,32},{8,40},{16,48},{24,56},{32,64},{40,72},{48,80},{56,88},{64,... | collective-permute-start | bytes 196616 | tf_op jit(solution)/shard_map/ppermute | solution.py:200
  34.1 2.4 %collective-permute-start.2 = (bf16[64,512]{1,0:T(8,128)(2,1)S(1)}, bf16[64,512]{1,0:T(8,128)(2,1)S(1)}, u32[]{:S(2)}, u32[]{:S(2)}) collective-permute-start(bf16[64,512]{1,0:T(8,128)(2,1)S(1)} %shard_map.59.refs_0_), channel_id=1, source_target_pairs={{0,96},{8,104},{16,112},{24,120},{32,0},{40,8},{48,16},{56,24},{64... | collective-permute-start | bytes 196616 | tf_op jit(solution)/shard_map/ppermute | solution.py:200
  36.5 12.1 %collective-permute-start.3 = (bf16[64,512]{1,0:T(8,128)(2,1)S(1)}, bf16[64,512]{1,0:T(8,128)(2,1)S(1)}, u32[]{:S(2)}, u32[]{:S(2)}) collective-permute-start(bf16[64,512]{1,0:T(8,128)(2,1)S(1)} %shard_map.59.refs_0_), channel_id=1, source_target_pairs={{0,64},{8,72},{16,80},{24,88},{32,96},{40,104},{48,112},{56,120},{... | collective-permute-start | bytes 196616 | tf_op jit(solution)/shard_map/ppermute | solution.py:200
  49.4 5.5 %all-to-all-start.1 = ((bf16[64,8,128]{2,1,0:T(8,128)(2,1)}), bf16[64,8,128]{2,1,0:T(8,128)(2,1)S(1)}, u32[]{:S(2)}, u32[]{:S(2)}) async-start(bf16[64,8,128]{2,1,0:T(8,128)(2,1)} %shard_map.56), calls=%async_computation.1 | async-start | bytes 262144 | tf_op jit(solution)/shard_map/all_to_all | solution.py:228
  55.0 3.5 %collective-permute-start.4 = (bf16[4,64,512]{2,1,0:T(8,128)(2,1)S(1)}, bf16[4,64,512]{2,1,0:T(8,128)(2,1)S(1)}, u32[]{:S(2)}, u32[]{:S(2)}) collective-permute-start(bf16[4,64,512]{2,1,0:T(8,128)(2,1)S(1)} %shard_map.60.refs_0_), channel_id=1, source_target_pairs={{0,8},{8,16},{16,24},{24,32},{32,40},{40,48},{48,56},{56,64},{64,7... | collective-permute-start | bytes 786440 | tf_op jit(solution)/shard_map/ppermute | solution.py:200
  58.5 4.0 %collective-permute-start.5 = (bf16[4,64,512]{2,1,0:T(8,128)(2,1)S(1)}, bf16[4,64,512]{2,1,0:T(8,128)(2,1)S(1)}, u32[]{:S(2)}, u32[]{:S(2)}) collective-permute-start(bf16[4,64,512]{2,1,0:T(8,128)(2,1)S(1)} %shard_map.60.refs_0_), channel_id=1, source_target_pairs={{0,120},{8,0},{16,8},{24,16},{32,24},{40,32},{48,40},{56,48},{64,5... | collective-permute-start | bytes 786440 | tf_op jit(solution)/shard_map/ppermute | solution.py:200
  62.5 2.8 %collective-permute-start.6 = (bf16[4,64,512]{2,1,0:T(8,128)(2,1)S(1)}, bf16[4,64,512]{2,1,0:T(8,128)(2,1)S(1)}, u32[]{:S(2)}, u32[]{:S(2)}) collective-permute-start(bf16[4,64,512]{2,1,0:T(8,128)(2,1)S(1)} %shard_map.60.refs_0_), channel_id=1, source_target_pairs={{0,16},{8,120},{16,32},{24,8},{32,48},{40,24},{48,64},{56,40},{64,... | collective-permute-start | bytes 786440 | tf_op jit(solution)/shard_map/ppermute | solution.py:200
  65.3 4.7 %all-to-all-done.1 = bf16[64,8,128]{2,1,0:T(8,128)(2,1)S(1)} async-done(((bf16[64,8,128]{2,1,0:T(8,128)(2,1)}), bf16[64,8,128]{2,1,0:T(8,128)(2,1)S(1)}, u32[]{:S(2)}, u32[]{:S(2)}) %all-to-all-start.1) | async-done | bytes 131104 | tf_op jit(solution)/shard_map/all_to_all | solution.py:228
  73.6 3.6 %all-to-all-start.2 = ((bf16[4,2,4,64,512]{4,3,2,1,0:T(8,128)(2,1)}), bf16[4,2,4,64,512]{4,3,2,1,0:T(8,128)(2,1)S(1)}, u32[]{:S(2)}, u32[]{:S(2)}) async-start(bf16[4,2,4,64,512]{4,3,2,1,0:T(8,128)(2,1)} %broadcast_in_dim.2), calls=%async_computation.2 | async-start | bytes 4194304 | tf_op jit(solution)/shard_map/all_to_all | solution.py:248
  78.1 2.3 %shard_map.61 = (bf16[8,64,512]{2,1,0:T(8,128)(2,1)}, bf16[8,64,512]{2,1,0:T(8,128)(2,1)}) custom-call(s32[1]{0:T(128)} %bitcast.5.place_ref, bf16[4,64,512]{2,1,0:T(8,128)(2,1)} %copy-done.6, bf16[4,64,512]{2,1,0:T(8,128)(2,1)} %copy-done.8, bf16[4,64,512]{2,1,0:T(8,128)(2,1)} %copy-done.9, bf16[4,64,512]{2,1,0:T(8,128)(2,1)} %copy-done.10), custom_call_target="tpu_custom_call" | custom-call | flops 8589934592 | bytes 2097152 | tf_op jit(solution)/shard_map/pallas_call | solution.py:131
  80.4 3.4 %collective-permute-start.7 = (bf16[8,64,512]{2,1,0:T(8,128)(2,1)}, bf16[8,64,512]{2,1,0:T(8,128)(2,1)S(1)}, u32[]{:S(2)}, u32[]{:S(2)}) collective-permute-start(bf16[8,64,512]{2,1,0:T(8,128)(2,1)} %get-tuple-element.19.refs_0_), channel_id=1, source_target_pairs={{0,128},{8,136},{16,144},{24,152},{32,160},{40,168},{48,176},{56,1... | collective-permute-start | bytes 1572872 | tf_op jit(solution)/shard_map/ppermute | solution.py:205
  83.8 2.5 %collective-permute-start.10 = (bf16[8,64,512]{2,1,0:T(8,128)(2,1)}, bf16[8,64,512]{2,1,0:T(8,128)(2,1)S(1)}, u32[]{:S(2)}, u32[]{:S(2)}) collective-permute-start(bf16[8,64,512]{2,1,0:T(8,128)(2,1)} %get-tuple-element.20.refs_1_), channel_id=1, source_target_pairs={{0,384},{8,392},{16,400},{24,408},{32,416},{40,424},{48,432},{56,4... | collective-permute-start | bytes 1572872 | tf_op jit(solution)/shard_map/ppermute | solution.py:205
  86.3 4.6 %collective-permute-start.8 = (bf16[8,64,512]{2,1,0:T(8,128)(2,1)}, bf16[8,64,512]{2,1,0:T(8,128)(2,1)}, u32[]{:S(2)}, u32[]{:S(2)}) collective-permute-start(bf16[8,64,512]{2,1,0:T(8,128)(2,1)} %get-tuple-element.20.refs_1_), channel_id=1, source_target_pairs={{0,128},{8,136},{16,144},{24,152},{32,160},{40,168},{48,176},{56,1... | collective-permute-start | bytes 1572872 | tf_op jit(solution)/shard_map/ppermute | solution.py:205
  90.9 1.9 %collective-permute-start.9 = (bf16[8,64,512]{2,1,0:T(8,128)(2,1)}, bf16[8,64,512]{2,1,0:T(8,128)(2,1)}, u32[]{:S(2)}, u32[]{:S(2)}) collective-permute-start(bf16[8,64,512]{2,1,0:T(8,128)(2,1)} %get-tuple-element.19.refs_0_), channel_id=1, source_target_pairs={{0,384},{8,392},{16,400},{24,408},{32,416},{40,424},{48,432},{56,4... | collective-permute-start | bytes 1572872 | tf_op jit(solution)/shard_map/ppermute | solution.py:205
  92.8 4.6 %collective-permute-done.7.refs_2_ = bf16[8,64,512]{2,1,0:T(8,128)(2,1)S(1)} collective-permute-done((bf16[8,64,512]{2,1,0:T(8,128)(2,1)}, bf16[8,64,512]{2,1,0:T(8,128)(2,1)S(1)}, u32[]{:S(2)}, u32[]{:S(2)}) %collective-permute-start.7) | collective-permute-done | bytes 524320 | tf_op jit(solution)/shard_map/ppermute | solution.py:205
  97.4 4.6 %collective-permute-start.11 = (bf16[8,64,512]{2,1,0:T(8,128)(2,1)S(1)}, bf16[8,64,512]{2,1,0:T(8,128)(2,1)}, u32[]{:S(2)}, u32[]{:S(2)}) collective-permute-start(bf16[8,64,512]{2,1,0:T(8,128)(2,1)S(1)} %collective-permute-done.7.refs_2_), channel_id=1, source_target_pairs={{0,128},{8,136},{16,144},{24,152},{32,160},{40,168},{48,176},{56,1... | collective-permute-start | bytes 1572872 | tf_op jit(solution)/shard_map/ppermute | solution.py:205
  102.0 1.9 %collective-permute-start.12 = (bf16[8,64,512]{2,1,0:T(8,128)(2,1)S(1)}, bf16[8,64,512]{2,1,0:T(8,128)(2,1)}, u32[]{:S(2)}, u32[]{:S(2)}) collective-permute-start(bf16[8,64,512]{2,1,0:T(8,128)(2,1)S(1)} %collective-permute-done.10.refs_5_), channel_id=1, source_target_pairs={{0,384},{8,392},{16,400},{24,408},{32,416},{40,424},{48,432},{56,4... | collective-permute-start | bytes 1572872 | tf_op jit(solution)/shard_map/ppermute | solution.py:205
  104.0 4.8 %collective-permute-done.8.refs_3_ = bf16[8,64,512]{2,1,0:T(8,128)(2,1)} collective-permute-done((bf16[8,64,512]{2,1,0:T(8,128)(2,1)}, bf16[8,64,512]{2,1,0:T(8,128)(2,1)}, u32[]{:S(2)}, u32[]{:S(2)}) %collective-permute-start.8) | collective-permute-done | bytes 524320 | tf_op jit(solution)/shard_map/ppermute | solution.py:205
  108.8 4.6 %collective-permute-done.9.refs_4_ = bf16[8,64,512]{2,1,0:T(8,128)(2,1)} collective-permute-done((bf16[8,64,512]{2,1,0:T(8,128)(2,1)}, bf16[8,64,512]{2,1,0:T(8,128)(2,1)}, u32[]{:S(2)}, u32[]{:S(2)}) %collective-permute-start.9) | collective-permute-done | bytes 524320 | tf_op jit(solution)/shard_map/ppermute | solution.py:205
  115.5 3.0 %shard_map.62.total_ref = f32[512,1024]{1,0:T(8,128)S(1)} custom-call(s32[1]{0:T(128)} %bitcast.place_ref, bf16[4,2,4,64,512]{4,3,2,1,0:T(8,128)(2,1)S(1)} %all-to-all-done.2.tokens_ref, bf16[8,64,512]{2,1,0:T(8,128)(2,1)S(1)} %copy-done.4, bf16[8,64,512]{2,1,0:T(8,128)(2,1)S(1)} %copy-done.5, bf16[8,64,512]{2,1,0:T(8,128)(2,1)S(1)} %collective-permute-done.7.refs_2_, ...), custom_call_target="tpu_custom_call" | custom-call | flops 1610612736 | bytes 4194304 | tf_op jit(solution)/shard_map/pallas_call | solution.py:29
  119.9 1.9 %shard_map.63 = (f32[256,1024]{1,0:T(8,128)S(1)}, bf16[256,1024]{1,0:T(8,128)(2,1)S(1)}) custom-call(s32[1]{0:T(128)} %bitcast.place_ref, bf16[4,2,4,64,512]{4,3,2,1,0:T(8,128)(2,1)S(1)} %all-to-all-done.2.tokens_ref, f32[512,1024]{1,0:T(8,128)S(1)} %shard_map.62.total_ref, bf16[8,64,512]{2,1,0:T(8,128)(2,1)} %collective-permute-done.11.first_ref, ...), custom_call_target="tpu_custom_call" | custom-call | flops 536870912 | bytes 4194304 | tf_op jit(solution)/shard_map/pallas_call | solution.py:29
  125.7 13.4 %all_to_all.20.parts_ref = bf16[4,64,1024]{2,1,0:T(8,128)(2,1)S(1)} all-to-all(bf16[4,64,1024]{2,1,0:T(8,128)(2,1)S(1)} %bitcast.8), channel_id=1, replica_groups={{0,2,4,6},{1,3,5,7},{8,10,12,14},{9,11,13,15},{16,18,20,22},{17,19,21,2..., dimensions={0} | all-to-all | bytes 1048576 | tf_op jit(solution)/shard_map/all_to_all | solution.py:264
  (45 shorter events, 16.7 us)
Async XLA Ops:
  0.0 26.7 %collective-permute-start = (bf16[64,512]{1,0:T(8,128)(2,1)}, bf16[64,512]{1,0:T(8,128)(2,1)S(1)}, u32[]{:S(2)}, u32[]{:S(2)}) collective-permute-start(bf16[64,512]{1,0:T(8,128)(2,1)} %bitcast.11), channel_id=1, source_target_pairs={{0,0},{1,1},{2,128},{3,129},{4,256},{5,257},{6,384},{7,385},{8,8},... | collective-permute-start | bytes 196616 | tf_op jit(solution)/shard_map/ppermute | solution.py:195
  4.3 1.0 copy-start
  5.4 1.0 copy-start.3
  7.6 41.1 %all-to-all-start = ((bf16[64,8,128]{2,1,0:T(8,128)(2,1)}), bf16[64,8,128]{2,1,0:T(8,128)(2,1)S(1)}, u32[]{:S(2)}, u32[]{:S(2)}) async-start(bf16[64,8,128]{2,1,0:T(8,128)(2,1)} %bitcast.2), calls=%async_computation | async-start | bytes 262144 | tf_op jit(solution)/shard_map/all_to_all | solution.py:224
  26.8 28.2 %collective-permute-start.1 = (bf16[64,512]{1,0:T(8,128)(2,1)S(1)}, bf16[64,512]{1,0:T(8,128)(2,1)S(1)}, u32[]{:S(2)}, u32[]{:S(2)}) collective-permute-start(bf16[64,512]{1,0:T(8,128)(2,1)S(1)} %shard_map.59.refs_0_), channel_id=1, source_target_pairs={{0,32},{8,40},{16,48},{24,56},{32,64},{40,72},{48,80},{56,88},{64,... | collective-permute-start | bytes 196616 | tf_op jit(solution)/shard_map/ppermute | solution.py:200
  34.1 20.9 %collective-permute-start.2 = (bf16[64,512]{1,0:T(8,128)(2,1)S(1)}, bf16[64,512]{1,0:T(8,128)(2,1)S(1)}, u32[]{:S(2)}, u32[]{:S(2)}) collective-permute-start(bf16[64,512]{1,0:T(8,128)(2,1)S(1)} %shard_map.59.refs_0_), channel_id=1, source_target_pairs={{0,96},{8,104},{16,112},{24,120},{32,0},{40,8},{48,16},{56,24},{64... | collective-permute-start | bytes 196616 | tf_op jit(solution)/shard_map/ppermute | solution.py:200
  36.5 18.5 %collective-permute-start.3 = (bf16[64,512]{1,0:T(8,128)(2,1)S(1)}, bf16[64,512]{1,0:T(8,128)(2,1)S(1)}, u32[]{:S(2)}, u32[]{:S(2)}) collective-permute-start(bf16[64,512]{1,0:T(8,128)(2,1)S(1)} %shard_map.59.refs_0_), channel_id=1, source_target_pairs={{0,64},{8,72},{16,80},{24,88},{32,96},{40,104},{48,112},{56,120},{... | collective-permute-start | bytes 196616 | tf_op jit(solution)/shard_map/ppermute | solution.py:200
  49.4 20.6 %all-to-all-start.1 = ((bf16[64,8,128]{2,1,0:T(8,128)(2,1)}), bf16[64,8,128]{2,1,0:T(8,128)(2,1)S(1)}, u32[]{:S(2)}, u32[]{:S(2)}) async-start(bf16[64,8,128]{2,1,0:T(8,128)(2,1)} %shard_map.56), calls=%async_computation.1 | async-start | bytes 262144 | tf_op jit(solution)/shard_map/all_to_all | solution.py:228
  54.9 15.1 %copy-start.1 = (bf16[512,512]{1,0:T(8,128)(2,1)S(1)}, bf16[512,512]{1,0:T(8,128)(2,1)}, u32[]{:S(2)}) copy-start(bf16[512,512]{1,0:T(8,128)(2,1)} %values_ref.3) | copy-start | bytes 1572868
  54.9 15.0 %copy-start.2 = (bf16[512,512]{1,0:T(8,128)(2,1)S(1)}, bf16[512,512]{1,0:T(8,128)(2,1)}, u32[]{:S(2)}) copy-start(bf16[512,512]{1,0:T(8,128)(2,1)} %queries_ref) | copy-start | bytes 1572868
  54.9 16.5 %copy-start.7 = (f32[512]{0:T(512)S(1)}, f32[512]{0:T(512)}, u32[]{:S(2)}) copy-start(f32[512]{0:T(512)} %param.9) | copy-start | bytes 6148
  55.0 17.0 %copy-start.6 = (bf16[4,64,512]{2,1,0:T(8,128)(2,1)}, bf16[4,64,512]{2,1,0:T(8,128)(2,1)S(1)}, u32[]{:S(2)}) copy-start(bf16[4,64,512]{2,1,0:T(8,128)(2,1)S(1)} %shard_map.60.refs_0_) | copy-start | bytes 786436
  55.0 22.2 %collective-permute-start.4 = (bf16[4,64,512]{2,1,0:T(8,128)(2,1)S(1)}, bf16[4,64,512]{2,1,0:T(8,128)(2,1)S(1)}, u32[]{:S(2)}, u32[]{:S(2)}) collective-permute-start(bf16[4,64,512]{2,1,0:T(8,128)(2,1)S(1)} %shard_map.60.refs_0_), channel_id=1, source_target_pairs={{0,8},{8,16},{16,24},{24,32},{32,40},{40,48},{48,56},{56,64},{64,7... | collective-permute-start | bytes 786440 | tf_op jit(solution)/shard_map/ppermute | solution.py:200
  58.5 18.7 %collective-permute-start.5 = (bf16[4,64,512]{2,1,0:T(8,128)(2,1)S(1)}, bf16[4,64,512]{2,1,0:T(8,128)(2,1)S(1)}, u32[]{:S(2)}, u32[]{:S(2)}) collective-permute-start(bf16[4,64,512]{2,1,0:T(8,128)(2,1)S(1)} %shard_map.60.refs_0_), channel_id=1, source_target_pairs={{0,120},{8,0},{16,8},{24,16},{32,24},{40,32},{48,40},{56,48},{64,5... | collective-permute-start | bytes 786440 | tf_op jit(solution)/shard_map/ppermute | solution.py:200
  62.5 14.7 %collective-permute-start.6 = (bf16[4,64,512]{2,1,0:T(8,128)(2,1)S(1)}, bf16[4,64,512]{2,1,0:T(8,128)(2,1)S(1)}, u32[]{:S(2)}, u32[]{:S(2)}) collective-permute-start(bf16[4,64,512]{2,1,0:T(8,128)(2,1)S(1)} %shard_map.60.refs_0_), channel_id=1, source_target_pairs={{0,16},{8,120},{16,32},{24,8},{32,48},{40,24},{48,64},{56,40},{64,... | collective-permute-start | bytes 786440 | tf_op jit(solution)/shard_map/ppermute | solution.py:200
  73.6 39.8 %all-to-all-start.2 = ((bf16[4,2,4,64,512]{4,3,2,1,0:T(8,128)(2,1)}), bf16[4,2,4,64,512]{4,3,2,1,0:T(8,128)(2,1)S(1)}, u32[]{:S(2)}, u32[]{:S(2)}) async-start(bf16[4,2,4,64,512]{4,3,2,1,0:T(8,128)(2,1)} %broadcast_in_dim.2), calls=%async_computation.2 | async-start | bytes 4194304 | tf_op jit(solution)/shard_map/all_to_all | solution.py:248
  80.4 17.0 %collective-permute-start.7 = (bf16[8,64,512]{2,1,0:T(8,128)(2,1)}, bf16[8,64,512]{2,1,0:T(8,128)(2,1)S(1)}, u32[]{:S(2)}, u32[]{:S(2)}) collective-permute-start(bf16[8,64,512]{2,1,0:T(8,128)(2,1)} %get-tuple-element.19.refs_0_), channel_id=1, source_target_pairs={{0,128},{8,136},{16,144},{24,152},{32,160},{40,168},{48,176},{56,1... | collective-permute-start | bytes 1572872 | tf_op jit(solution)/shard_map/ppermute | solution.py:205
  83.8 18.2 %collective-permute-start.10 = (bf16[8,64,512]{2,1,0:T(8,128)(2,1)}, bf16[8,64,512]{2,1,0:T(8,128)(2,1)S(1)}, u32[]{:S(2)}, u32[]{:S(2)}) collective-permute-start(bf16[8,64,512]{2,1,0:T(8,128)(2,1)} %get-tuple-element.20.refs_1_), channel_id=1, source_target_pairs={{0,384},{8,392},{16,400},{24,408},{32,416},{40,424},{48,432},{56,4... | collective-permute-start | bytes 1572872 | tf_op jit(solution)/shard_map/ppermute | solution.py:205
  86.3 22.5 %collective-permute-start.8 = (bf16[8,64,512]{2,1,0:T(8,128)(2,1)}, bf16[8,64,512]{2,1,0:T(8,128)(2,1)}, u32[]{:S(2)}, u32[]{:S(2)}) collective-permute-start(bf16[8,64,512]{2,1,0:T(8,128)(2,1)} %get-tuple-element.20.refs_1_), channel_id=1, source_target_pairs={{0,128},{8,136},{16,144},{24,152},{32,160},{40,168},{48,176},{56,1... | collective-permute-start | bytes 1572872 | tf_op jit(solution)/shard_map/ppermute | solution.py:205
  90.9 22.4 %collective-permute-start.9 = (bf16[8,64,512]{2,1,0:T(8,128)(2,1)}, bf16[8,64,512]{2,1,0:T(8,128)(2,1)}, u32[]{:S(2)}, u32[]{:S(2)}) collective-permute-start(bf16[8,64,512]{2,1,0:T(8,128)(2,1)} %get-tuple-element.19.refs_0_), channel_id=1, source_target_pairs={{0,384},{8,392},{16,400},{24,408},{32,416},{40,424},{48,432},{56,4... | collective-permute-start | bytes 1572872 | tf_op jit(solution)/shard_map/ppermute | solution.py:205
  97.4 21.1 %collective-permute-start.11 = (bf16[8,64,512]{2,1,0:T(8,128)(2,1)S(1)}, bf16[8,64,512]{2,1,0:T(8,128)(2,1)}, u32[]{:S(2)}, u32[]{:S(2)}) collective-permute-start(bf16[8,64,512]{2,1,0:T(8,128)(2,1)S(1)} %collective-permute-done.7.refs_2_), channel_id=1, source_target_pairs={{0,128},{8,136},{16,144},{24,152},{32,160},{40,168},{48,176},{56,1... | collective-permute-start | bytes 1572872 | tf_op jit(solution)/shard_map/ppermute | solution.py:205
  102.0 17.9 %collective-permute-start.12 = (bf16[8,64,512]{2,1,0:T(8,128)(2,1)S(1)}, bf16[8,64,512]{2,1,0:T(8,128)(2,1)}, u32[]{:S(2)}, u32[]{:S(2)}) collective-permute-start(bf16[8,64,512]{2,1,0:T(8,128)(2,1)S(1)} %collective-permute-done.10.refs_5_), channel_id=1, source_target_pairs={{0,384},{8,392},{16,400},{24,408},{32,416},{40,424},{48,432},{56,4... | collective-permute-start | bytes 1572872 | tf_op jit(solution)/shard_map/ppermute | solution.py:205
  113.4 1.0 copy-start.4
  121.8 3.8 %collective-permute-start.13 = (bf16[256,1024]{1,0:T(8,128)(2,1)S(1)}, bf16[256,1024]{1,0:T(8,128)(2,1)S(1)}, u32[]{:S(2)}, u32[]{:S(2)}) collective-permute-start(bf16[256,1024]{1,0:T(8,128)(2,1)S(1)} %get-tuple-element.22), channel_id=1, source_target_pairs={{0,1},{1,0},{2,3},{3,2},{4,5},{5,4},{6,7},{7,6},{8,9},{9,8},{10,11... | collective-permute-start | bytes 1572872 | tf_op jit(solution)/shard_map/ppermute | solution.py:262
  (4 other events, 3.4 us)

commit v4 on v3

--- a/solution.py
+++ b/solution.py
@@ -45,13 +45,38 @@
     return [slice(h * DH, (h + 1) * DH) for h in range(ref.shape[1] // DH)]
 
 
-def memory_kernel(keys_ref, values_ref, key_ref, memory_ref):
-    for cols in heads(keys_ref):
-        key = feature(keys_ref[:, cols])
+def memory_kernel(keys_ref, values_ref, key_ref, memory_ref, raw_ref, held_ref, arrived):
+    copies = []
+    for head, cols in enumerate(heads(keys_ref)):
+        for side, (source, target) in enumerate(((keys_ref, raw_ref), (values_ref, held_ref))):
+            copies.append(pltpu.make_async_copy(source.at[:, cols], target.at[:, cols], arrived.at[head, side]))
+            copies[-1].start()
+    for head, cols in enumerate(heads(keys_ref)):
+        copies[2 * head].wait()
+        key = feature(raw_ref[:, cols])
         key_ref[:, cols] = key
+        copies[2 * head + 1].wait()
         memory_ref[cols, :] = lax.dot_general(
-            key, values_ref[:, cols], (((0,), (0,)), ((), ())), preferred_element_type=f32
+            key, held_ref[:, cols], (((0,), (0,)), ((), ())), preferred_element_type=f32
         ).astype(bf16)
+
+
+def memories(keys, values):
+    rows, width = keys.shape
+    anywhere = pl.BlockSpec(memory_space=pl.ANY)
+    return pl.pallas_call(
+        memory_kernel,
+        in_specs=[anywhere, anywhere],
+        out_specs=[VMEM, VMEM],
+        out_shape=[jax.ShapeDtypeStruct(keys.shape, bf16), jax.ShapeDtypeStruct((width, DH), bf16)],
+        scratch_shapes=[
+            pltpu.VMEM(keys.shape, bf16),
+            pltpu.VMEM(keys.shape, bf16),
+            pltpu.SemaphoreType.DMA((width // DH, 2)),
+        ],
+        compiler_params=pltpu.CompilerParams(vmem_limit_bytes=56 << 20),
+        cost_estimate=pl.CostEstimate(flops=1 << 26, bytes_accessed=2 << 20, transcendentals=1 << 18),
+    )(keys, values)
 
 
 def local_kernel(queries_ref, key_ref, values_ref, query_ref, attended_ref):
@@ -220,7 +245,7 @@
     own = to_plane(out_weight.T)
     (own,) = call(pass_kernel, [shape(own.shape, bf16)], 1<<33, own)
     far = [along_z(own, lambda z, s=s: s) for s in (NL, -NL, 2 * NL)]
-    key, memory = call(memory_kernel, [shape((rows, width), bf16), shape((width, DH), bf16)], 1 << 26, keys, values)
+    key, memory = memories(keys, values)
     pieces = lax.all_to_all(memory.reshape(blocks, -1, DH), "seq", 0, 0, tiled=True)
     (stack,) = call(stack_kernel, [shape((NL, *own.shape), bf16)], 1<<33, own, *far)
     near = [along_z(stack, s) for s in (lambda z: 1, lambda z: -1, lambda z: 2 - 4 * (z % 2))]
@@ -249,7 +274,7 @@
 
     columns = NZ * own.shape[0]
     halves = (low, high, ahead_low, ahead_high, behind_low, behind_high)
-    total = placed_call(near_kernel, shape((rows, columns), f32), 3 << 29, y, tokens, *halves)
+    total = placed_call(near_kernel, shape((rows, columns), f32), 1 << 33, y, tokens, *halves)
     mine, theirs = placed_call(
         far_kernel,
         [shape((rows // 2, columns), f32), shape((rows // 2, columns), bf16)],

time: 141 us -> 139 us (0.986)
  local copies, waits for them, and re-layouts: 6.62 us -> 4.56 us
    pallas_call x0 -> x1, Pallas kernels: none -> 2.84 us  [memories(): pl.pallas_call(memory_kernel, in_specs=[anywhere, anywhere], out_specs=[V...]
    unnamed x22 -> x20, local copies, waits for them, and re-layouts: 5.03 us -> 2.97 us
    pallas_call x7 -> x6, Pallas kernels: 4.33 us -> 3.12 us  [call(): pl.pallas_call(kernel, in_specs=[VMEM] * len(args), out_specs=[VMEM] * le...]
  transfers between devices with their start and end apart: 17 -> 17, of which waited for: 6 -> 6; matrix products, arithmetic and copies ran while one was open for 1% -> 1% of each run, Pallas kernels for 7% -> 8%
where the time goes in v4:
time: 139 us; the launch traced here: 138 us
  starting transfers between devices  85.5 us (62%)
  waiting for transfers between devices  21.5 us (15%)
  blocking collectives  13.4 us (10%)
  Pallas kernels  12.9 us (9%)
  local copies, waits for them, and re-layouts  4.56 us (3%)
    ppermute x6, starting transfers between devices, along_z(): return lax.ppermute(block, 'seq', pairs)  32.1 us
    all_to_all x1, starting transfers between devices, body(): lax.all_to_all(memory.reshape(blocks, -1, DH), 'seq', 0, 0, tiled=True)  19.1 us
    ppermute x6, starting transfers between devices, along_y(): return lax.ppermute(block, 'seq', pairs)  18.9 us
    ppermute x6, waiting for transfers between devices, along_y(): return lax.ppermute(block, 'seq', pairs)  14.9 us
    all_to_all x1, blocking collectives, body(): lax.all_to_all(summed.reshape(NX, rows // 8, -1), 'head', 0, 0, tiled=Tru...  13.4 us
    all_to_all x1, starting transfers between devices, body(): prior = lax.all_to_all(sums, 'seq', 0, 0, tiled=True).reshape(width, DH)  5.51 us
    all_to_all x1, waiting for transfers between devices, body(): prior = lax.all_to_all(sums, 'seq', 0, 0, tiled=True).reshape(width, DH)  4.67 us
    pallas_call x3, Pallas kernels, placed_call(): pl.pallas_call(kernel, in_specs=[pl.BlockSpec(memory_space=pltpu.SMEM)] +...  4.58 us
  transfers between devices with their start and end apart: 17, of which 6 were waited for; matrix products, arithmetic and copies ran while one was open for 1% of the time, Pallas kernels for 8%

profile of v4, /device:TPU:24, one launch (start us, length us, event | category | flops | bytes accessed | tf_op | source)
XLA Modules:
  0.0 138.2 jit_solution(14940498130331162497)
XLA Ops:
  0.0 4.3 %collective-permute-start = (bf16[64,512]{1,0:T(8,128)(2,1)}, bf16[64,512]{1,0:T(8,128)(2,1)S(1)}, u32[]{:S(2)}, u32[]{:S(2)}) collective-permute-start(bf16[64,512]{1,0:T(8,128)(2,1)} %bitcast.12), channel_id=1, source_target_pairs={{0,0},{1,1},{2,128},{3,129},{4,256},{5,257},{6,384},{7,385},{8,8},... | collective-permute-start | bytes 196616 | tf_op jit(solution)/shard_map/ppermute | solution.py:220
  4.3 2.8 %shard_map.55 = (bf16[512,512]{1,0:T(8,128)(2,1)}, bf16[512,128]{1,0:T(8,128)(2,1)}) custom-call(bf16[512,512]{1,0:T(8,128)(2,1)} %keys_ref.1, bf16[512,512]{1,0:T(8,128)(2,1)} %values_ref.3), custom_call_target="tpu_custom_call" | custom-call | flops 67108864 | bytes 2097152 | tf_op jit(solution)/shard_map/pallas_call | solution.py:67
  7.2 19.1 %all-to-all-start = ((bf16[64,8,128]{2,1,0:T(8,128)(2,1)}), bf16[64,8,128]{2,1,0:T(8,128)(2,1)S(1)}, u32[]{:S(2)}, u32[]{:S(2)}) async-start(bf16[64,8,128]{2,1,0:T(8,128)(2,1)} %bitcast.11), calls=%async_computation | async-start | bytes 262144 | tf_op jit(solution)/shard_map/all_to_all | solution.py:249
  26.3 7.3 %collective-permute-start.1 = (bf16[64,512]{1,0:T(8,128)(2,1)S(1)}, bf16[64,512]{1,0:T(8,128)(2,1)S(1)}, u32[]{:S(2)}, u32[]{:S(2)}) collective-permute-start(bf16[64,512]{1,0:T(8,128)(2,1)S(1)} %shard_map.59.refs_0_), channel_id=1, source_target_pairs={{0,32},{8,40},{16,48},{24,56},{32,64},{40,72},{48,80},{56,88},{64,... | collective-permute-start | bytes 196616 | tf_op jit(solution)/shard_map/ppermute | solution.py:225
  33.6 2.4 %collective-permute-start.2 = (bf16[64,512]{1,0:T(8,128)(2,1)S(1)}, bf16[64,512]{1,0:T(8,128)(2,1)S(1)}, u32[]{:S(2)}, u32[]{:S(2)}) collective-permute-start(bf16[64,512]{1,0:T(8,128)(2,1)S(1)} %shard_map.59.refs_0_), channel_id=1, source_target_pairs={{0,96},{8,104},{16,112},{24,120},{32,0},{40,8},{48,16},{56,24},{64... | collective-permute-start | bytes 196616 | tf_op jit(solution)/shard_map/ppermute | solution.py:225
  36.1 12.1 %collective-permute-start.3 = (bf16[64,512]{1,0:T(8,128)(2,1)S(1)}, bf16[64,512]{1,0:T(8,128)(2,1)S(1)}, u32[]{:S(2)}, u32[]{:S(2)}) collective-permute-start(bf16[64,512]{1,0:T(8,128)(2,1)S(1)} %shard_map.59.refs_0_), channel_id=1, source_target_pairs={{0,64},{8,72},{16,80},{24,88},{32,96},{40,104},{48,112},{56,120},{... | collective-permute-start | bytes 196616 | tf_op jit(solution)/shard_map/ppermute | solution.py:225
  49.0 5.5 %all-to-all-start.1 = ((bf16[64,8,128]{2,1,0:T(8,128)(2,1)}), bf16[64,8,128]{2,1,0:T(8,128)(2,1)S(1)}, u32[]{:S(2)}, u32[]{:S(2)}) async-start(bf16[64,8,128]{2,1,0:T(8,128)(2,1)} %shard_map.56), calls=%async_computation.1 | async-start | bytes 262144 | tf_op jit(solution)/shard_map/all_to_all | solution.py:253
  54.6 3.5 %collective-permute-start.4 = (bf16[4,64,512]{2,1,0:T(8,128)(2,1)S(1)}, bf16[4,64,512]{2,1,0:T(8,128)(2,1)S(1)}, u32[]{:S(2)}, u32[]{:S(2)}) collective-permute-start(bf16[4,64,512]{2,1,0:T(8,128)(2,1)S(1)} %shard_map.60.refs_0_), channel_id=1, source_target_pairs={{0,8},{8,16},{16,24},{24,32},{32,40},{40,48},{48,56},{56,64},{64,7... | collective-permute-start | bytes 786440 | tf_op jit(solution)/shard_map/ppermute | solution.py:225
  58.1 4.0 %collective-permute-start.5 = (bf16[4,64,512]{2,1,0:T(8,128)(2,1)S(1)}, bf16[4,64,512]{2,1,0:T(8,128)(2,1)S(1)}, u32[]{:S(2)}, u32[]{:S(2)}) collective-permute-start(bf16[4,64,512]{2,1,0:T(8,128)(2,1)S(1)} %shard_map.60.refs_0_), channel_id=1, source_target_pairs={{0,120},{8,0},{16,8},{24,16},{32,24},{40,32},{48,40},{56,48},{64,5... | collective-permute-start | bytes 786440 | tf_op jit(solution)/shard_map/ppermute | solution.py:225
  62.1 2.8 %collective-permute-start.6 = (bf16[4,64,512]{2,1,0:T(8,128)(2,1)S(1)}, bf16[4,64,512]{2,1,0:T(8,128)(2,1)S(1)}, u32[]{:S(2)}, u32[]{:S(2)}) collective-permute-start(bf16[4,64,512]{2,1,0:T(8,128)(2,1)S(1)} %shard_map.60.refs_0_), channel_id=1, source_target_pairs={{0,16},{8,120},{16,32},{24,8},{32,48},{40,24},{48,64},{56,40},{64,... | collective-permute-start | bytes 786440 | tf_op jit(solution)/shard_map/ppermute | solution.py:225
  64.9 4.7 %all-to-all-done.1 = bf16[64,8,128]{2,1,0:T(8,128)(2,1)S(1)} async-done(((bf16[64,8,128]{2,1,0:T(8,128)(2,1)}), bf16[64,8,128]{2,1,0:T(8,128)(2,1)S(1)}, u32[]{:S(2)}, u32[]{:S(2)}) %all-to-all-start.1) | async-done | bytes 131104 | tf_op jit(solution)/shard_map/all_to_all | solution.py:253
  73.2 3.6 %all-to-all-start.2 = ((bf16[4,2,4,64,512]{4,3,2,1,0:T(8,128)(2,1)}), bf16[4,2,4,64,512]{4,3,2,1,0:T(8,128)(2,1)S(1)}, u32[]{:S(2)}, u32[]{:S(2)}) async-start(bf16[4,2,4,64,512]{4,3,2,1,0:T(8,128)(2,1)} %broadcast_in_dim.2), calls=%async_computation.2 | async-start | bytes 4194304 | tf_op jit(solution)/shard_map/all_to_all | solution.py:273
  77.7 2.3 %shard_map.61 = (bf16[8,64,512]{2,1,0:T(8,128)(2,1)}, bf16[8,64,512]{2,1,0:T(8,128)(2,1)}) custom-call(s32[1]{0:T(128)} %bitcast.5.place_ref, bf16[4,64,512]{2,1,0:T(8,128)(2,1)} %copy-done.5, bf16[4,64,512]{2,1,0:T(8,128)(2,1)} %copy-done.7, bf16[4,64,512]{2,1,0:T(8,128)(2,1)} %copy-done.8, bf16[4,64,512]{2,1,0:T(8,128)(2,1)} %copy-done.9), custom_call_target="tpu_custom_call" | custom-call | flops 8589934592 | bytes 2097152 | tf_op jit(solution)/shard_map/pallas_call | solution.py:156
  80.1 3.4 %collective-permute-start.7 = (bf16[8,64,512]{2,1,0:T(8,128)(2,1)}, bf16[8,64,512]{2,1,0:T(8,128)(2,1)}, u32[]{:S(2)}, u32[]{:S(2)}) collective-permute-start(bf16[8,64,512]{2,1,0:T(8,128)(2,1)} %get-tuple-element.19.refs_0_), channel_id=1, source_target_pairs={{0,128},{8,136},{16,144},{24,152},{32,160},{40,168},{48,176},{56,1... | collective-permute-start | bytes 1572872 | tf_op jit(solution)/shard_map/ppermute | solution.py:230
  83.5 2.5 %collective-permute-start.10 = (bf16[8,64,512]{2,1,0:T(8,128)(2,1)}, bf16[8,64,512]{2,1,0:T(8,128)(2,1)}, u32[]{:S(2)}, u32[]{:S(2)}) collective-permute-start(bf16[8,64,512]{2,1,0:T(8,128)(2,1)} %get-tuple-element.20.refs_1_), channel_id=1, source_target_pairs={{0,384},{8,392},{16,400},{24,408},{32,416},{40,424},{48,432},{56,4... | collective-permute-start | bytes 1572872 | tf_op jit(solution)/shard_map/ppermute | solution.py:230
  85.9 4.6 %collective-permute-start.8 = (bf16[8,64,512]{2,1,0:T(8,128)(2,1)}, bf16[8,64,512]{2,1,0:T(8,128)(2,1)}, u32[]{:S(2)}, u32[]{:S(2)}) collective-permute-start(bf16[8,64,512]{2,1,0:T(8,128)(2,1)} %get-tuple-element.20.refs_1_), channel_id=1, source_target_pairs={{0,128},{8,136},{16,144},{24,152},{32,160},{40,168},{48,176},{56,1... | collective-permute-start | bytes 1572872 | tf_op jit(solution)/shard_map/ppermute | solution.py:230
  90.5 1.9 %collective-permute-start.9 = (bf16[8,64,512]{2,1,0:T(8,128)(2,1)}, bf16[8,64,512]{2,1,0:T(8,128)(2,1)}, u32[]{:S(2)}, u32[]{:S(2)}) collective-permute-start(bf16[8,64,512]{2,1,0:T(8,128)(2,1)} %get-tuple-element.19.refs_0_), channel_id=1, source_target_pairs={{0,384},{8,392},{16,400},{24,408},{32,416},{40,424},{48,432},{56,4... | collective-permute-start | bytes 1572872 | tf_op jit(solution)/shard_map/ppermute | solution.py:230
  92.5 4.7 %collective-permute-done.7.refs_2_ = bf16[8,64,512]{2,1,0:T(8,128)(2,1)} collective-permute-done((bf16[8,64,512]{2,1,0:T(8,128)(2,1)}, bf16[8,64,512]{2,1,0:T(8,128)(2,1)}, u32[]{:S(2)}, u32[]{:S(2)}) %collective-permute-start.7) | collective-permute-done | bytes 524320 | tf_op jit(solution)/shard_map/ppermute | solution.py:230
  97.1 4.6 %collective-permute-start.11 = (bf16[8,64,512]{2,1,0:T(8,128)(2,1)}, bf16[8,64,512]{2,1,0:T(8,128)(2,1)S(1)}, u32[]{:S(2)}, u32[]{:S(2)}) collective-permute-start(bf16[8,64,512]{2,1,0:T(8,128)(2,1)} %collective-permute-done.7.refs_2_), channel_id=1, source_target_pairs={{0,128},{8,136},{16,144},{24,152},{32,160},{40,168},{48,176},{56,1... | collective-permute-start | bytes 1572872 | tf_op jit(solution)/shard_map/ppermute | solution.py:230
  103.7 4.7 %collective-permute-done.8.refs_3_ = bf16[8,64,512]{2,1,0:T(8,128)(2,1)} collective-permute-done((bf16[8,64,512]{2,1,0:T(8,128)(2,1)}, bf16[8,64,512]{2,1,0:T(8,128)(2,1)}, u32[]{:S(2)}, u32[]{:S(2)}) %collective-permute-start.8) | collective-permute-done | bytes 524320 | tf_op jit(solution)/shard_map/ppermute | solution.py:230
  108.4 4.5 %collective-permute-done.9.refs_4_ = bf16[8,64,512]{2,1,0:T(8,128)(2,1)} collective-permute-done((bf16[8,64,512]{2,1,0:T(8,128)(2,1)}, bf16[8,64,512]{2,1,0:T(8,128)(2,1)}, u32[]{:S(2)}, u32[]{:S(2)}) %collective-permute-start.9) | collective-permute-done | bytes 524320 | tf_op jit(solution)/shard_map/ppermute | solution.py:230
  114.9 3.3 %shard_map.62.total_ref = f32[512,1024]{1,0:T(8,128)S(1)} custom-call(s32[1]{0:T(128)} %bitcast.place_ref, bf16[4,2,4,64,512]{4,3,2,1,0:T(8,128)(2,1)S(1)} %all-to-all-done.2.tokens_ref, bf16[8,64,512]{2,1,0:T(8,128)(2,1)S(1)} %copy-done.3, bf16[8,64,512]{2,1,0:T(8,128)(2,1)S(1)} %copy-done.4, bf16[8,64,512]{2,1,0:T(8,128)(2,1)} %collective-permute-done.7.refs_2_, ...), custom_call_target="tpu_custom_call" | custom-call | flops 8589934592 | bytes 4194304 | tf_op jit(solution)/shard_map/pallas_call | solution.py:29
  120.1 1.9 %collective-permute-start.13 = (bf16[256,1024]{1,0:T(8,128)(2,1)S(1)}, bf16[256,1024]{1,0:T(8,128)(2,1)S(1)}, u32[]{:S(2)}, u32[]{:S(2)}) collective-permute-start(bf16[256,1024]{1,0:T(8,128)(2,1)S(1)} %get-tuple-element.22), channel_id=1, source_target_pairs={{0,1},{1,0},{2,3},{3,2},{4,5},{5,4},{6,7},{7,6},{8,9},{9,8},{10,11... | collective-permute-start | bytes 1572872 | tf_op jit(solution)/shard_map/ppermute | solution.py:287
  124.0 13.4 %all_to_all.20.parts_ref = bf16[4,64,1024]{2,1,0:T(8,128)(2,1)S(1)} all-to-all(bf16[4,64,1024]{2,1,0:T(8,128)(2,1)S(1)} %bitcast.8), channel_id=1, replica_groups={{0,2,4,6},{1,3,5,7},{8,10,12,14},{9,11,13,15},{16,18,20,22},{17,19,21,2..., dimensions={0} | all-to-all | bytes 1048576 | tf_op jit(solution)/shard_map/all_to_all | solution.py:289
  (43 shorter events, 13.8 us)
Async XLA Ops:
  0.0 26.3 %collective-permute-start = (bf16[64,512]{1,0:T(8,128)(2,1)}, bf16[64,512]{1,0:T(8,128)(2,1)S(1)}, u32[]{:S(2)}, u32[]{:S(2)}) collective-permute-start(bf16[64,512]{1,0:T(8,128)(2,1)} %bitcast.12), channel_id=1, source_target_pairs={{0,0},{1,1},{2,128},{3,129},{4,256},{5,257},{6,384},{7,385},{8,8},... | collective-permute-start | bytes 196616 | tf_op jit(solution)/shard_map/ppermute | solution.py:220
  7.2 41.1 %all-to-all-start = ((bf16[64,8,128]{2,1,0:T(8,128)(2,1)}), bf16[64,8,128]{2,1,0:T(8,128)(2,1)S(1)}, u32[]{:S(2)}, u32[]{:S(2)}) async-start(bf16[64,8,128]{2,1,0:T(8,128)(2,1)} %bitcast.11), calls=%async_computation | async-start | bytes 262144 | tf_op jit(solution)/shard_map/all_to_all | solution.py:249
  26.3 28.2 %collective-permute-start.1 = (bf16[64,512]{1,0:T(8,128)(2,1)S(1)}, bf16[64,512]{1,0:T(8,128)(2,1)S(1)}, u32[]{:S(2)}, u32[]{:S(2)}) collective-permute-start(bf16[64,512]{1,0:T(8,128)(2,1)S(1)} %shard_map.59.refs_0_), channel_id=1, source_target_pairs={{0,32},{8,40},{16,48},{24,56},{32,64},{40,72},{48,80},{56,88},{64,... | collective-permute-start | bytes 196616 | tf_op jit(solution)/shard_map/ppermute | solution.py:225
  33.6 20.9 %collective-permute-start.2 = (bf16[64,512]{1,0:T(8,128)(2,1)S(1)}, bf16[64,512]{1,0:T(8,128)(2,1)S(1)}, u32[]{:S(2)}, u32[]{:S(2)}) collective-permute-start(bf16[64,512]{1,0:T(8,128)(2,1)S(1)} %shard_map.59.refs_0_), channel_id=1, source_target_pairs={{0,96},{8,104},{16,112},{24,120},{32,0},{40,8},{48,16},{56,24},{64... | collective-permute-start | bytes 196616 | tf_op jit(solution)/shard_map/ppermute | solution.py:225
  36.1 18.5 %collective-permute-start.3 = (bf16[64,512]{1,0:T(8,128)(2,1)S(1)}, bf16[64,512]{1,0:T(8,128)(2,1)S(1)}, u32[]{:S(2)}, u32[]{:S(2)}) collective-permute-start(bf16[64,512]{1,0:T(8,128)(2,1)S(1)} %shard_map.59.refs_0_), channel_id=1, source_target_pairs={{0,64},{8,72},{16,80},{24,88},{32,96},{40,104},{48,112},{56,120},{... | collective-permute-start | bytes 196616 | tf_op jit(solution)/shard_map/ppermute | solution.py:225
  49.0 20.6 %all-to-all-start.1 = ((bf16[64,8,128]{2,1,0:T(8,128)(2,1)}), bf16[64,8,128]{2,1,0:T(8,128)(2,1)S(1)}, u32[]{:S(2)}, u32[]{:S(2)}) async-start(bf16[64,8,128]{2,1,0:T(8,128)(2,1)} %shard_map.56), calls=%async_computation.1 | async-start | bytes 262144 | tf_op jit(solution)/shard_map/all_to_all | solution.py:253
  54.5 15.1 %copy-start = (bf16[512,512]{1,0:T(8,128)(2,1)S(1)}, bf16[512,512]{1,0:T(8,128)(2,1)}, u32[]{:S(2)}) copy-start(bf16[512,512]{1,0:T(8,128)(2,1)} %values_ref.3) | copy-start | bytes 1572868
  54.5 15.1 %copy-start.1 = (bf16[512,512]{1,0:T(8,128)(2,1)S(1)}, bf16[512,512]{1,0:T(8,128)(2,1)}, u32[]{:S(2)}) copy-start(bf16[512,512]{1,0:T(8,128)(2,1)} %queries_ref) | copy-start | bytes 1572868
  54.5 15.0 %copy-start.2 = (bf16[512,512]{1,0:T(8,128)(2,1)S(1)}, bf16[512,512]{1,0:T(8,128)(2,1)}, u32[]{:S(2)}) copy-start(bf16[512,512]{1,0:T(8,128)(2,1)} %get-tuple-element.16.key_ref) | copy-start | bytes 1572868
  54.5 16.5 %copy-start.6 = (f32[512]{0:T(512)S(1)}, f32[512]{0:T(512)}, u32[]{:S(2)}) copy-start(f32[512]{0:T(512)} %param.9) | copy-start | bytes 6148
  54.6 17.0 %copy-start.5 = (bf16[4,64,512]{2,1,0:T(8,128)(2,1)}, bf16[4,64,512]{2,1,0:T(8,128)(2,1)S(1)}, u32[]{:S(2)}) copy-start(bf16[4,64,512]{2,1,0:T(8,128)(2,1)S(1)} %shard_map.60.refs_0_) | copy-start | bytes 786436
  54.6 22.2 %collective-permute-start.4 = (bf16[4,64,512]{2,1,0:T(8,128)(2,1)S(1)}, bf16[4,64,512]{2,1,0:T(8,128)(2,1)S(1)}, u32[]{:S(2)}, u32[]{:S(2)}) collective-permute-start(bf16[4,64,512]{2,1,0:T(8,128)(2,1)S(1)} %shard_map.60.refs_0_), channel_id=1, source_target_pairs={{0,8},{8,16},{16,24},{24,32},{32,40},{40,48},{48,56},{56,64},{64,7... | collective-permute-start | bytes 786440 | tf_op jit(solution)/shard_map/ppermute | solution.py:225
  58.1 18.7 %collective-permute-start.5 = (bf16[4,64,512]{2,1,0:T(8,128)(2,1)S(1)}, bf16[4,64,512]{2,1,0:T(8,128)(2,1)S(1)}, u32[]{:S(2)}, u32[]{:S(2)}) collective-permute-start(bf16[4,64,512]{2,1,0:T(8,128)(2,1)S(1)} %shard_map.60.refs_0_), channel_id=1, source_target_pairs={{0,120},{8,0},{16,8},{24,16},{32,24},{40,32},{48,40},{56,48},{64,5... | collective-permute-start | bytes 786440 | tf_op jit(solution)/shard_map/ppermute | solution.py:225
  62.1 14.7 %collective-permute-start.6 = (bf16[4,64,512]{2,1,0:T(8,128)(2,1)S(1)}, bf16[4,64,512]{2,1,0:T(8,128)(2,1)S(1)}, u32[]{:S(2)}, u32[]{:S(2)}) collective-permute-start(bf16[4,64,512]{2,1,0:T(8,128)(2,1)S(1)} %shard_map.60.refs_0_), channel_id=1, source_target_pairs={{0,16},{8,120},{16,32},{24,8},{32,48},{40,24},{48,64},{56,40},{64,... | collective-permute-start | bytes 786440 | tf_op jit(solution)/shard_map/ppermute | solution.py:225
  73.2 39.7 %all-to-all-start.2 = ((bf16[4,2,4,64,512]{4,3,2,1,0:T(8,128)(2,1)}), bf16[4,2,4,64,512]{4,3,2,1,0:T(8,128)(2,1)S(1)}, u32[]{:S(2)}, u32[]{:S(2)}) async-start(bf16[4,2,4,64,512]{4,3,2,1,0:T(8,128)(2,1)} %broadcast_in_dim.2), calls=%async_computation.2 | async-start | bytes 4194304 | tf_op jit(solution)/shard_map/all_to_all | solution.py:273
  80.1 17.1 %collective-permute-start.7 = (bf16[8,64,512]{2,1,0:T(8,128)(2,1)}, bf16[8,64,512]{2,1,0:T(8,128)(2,1)}, u32[]{:S(2)}, u32[]{:S(2)}) collective-permute-start(bf16[8,64,512]{2,1,0:T(8,128)(2,1)} %get-tuple-element.19.refs_0_), channel_id=1, source_target_pairs={{0,128},{8,136},{16,144},{24,152},{32,160},{40,168},{48,176},{56,1... | collective-permute-start | bytes 1572872 | tf_op jit(solution)/shard_map/ppermute | solution.py:230
  83.5 18.3 %collective-permute-start.10 = (bf16[8,64,512]{2,1,0:T(8,128)(2,1)}, bf16[8,64,512]{2,1,0:T(8,128)(2,1)}, u32[]{:S(2)}, u32[]{:S(2)}) collective-permute-start(bf16[8,64,512]{2,1,0:T(8,128)(2,1)} %get-tuple-element.20.refs_1_), channel_id=1, source_target_pairs={{0,384},{8,392},{16,400},{24,408},{32,416},{40,424},{48,432},{56,4... | collective-permute-start | bytes 1572872 | tf_op jit(solution)/shard_map/ppermute | solution.py:230
  85.9 22.4 %collective-permute-start.8 = (bf16[8,64,512]{2,1,0:T(8,128)(2,1)}, bf16[8,64,512]{2,1,0:T(8,128)(2,1)}, u32[]{:S(2)}, u32[]{:S(2)}) collective-permute-start(bf16[8,64,512]{2,1,0:T(8,128)(2,1)} %get-tuple-element.20.refs_1_), channel_id=1, source_target_pairs={{0,128},{8,136},{16,144},{24,152},{32,160},{40,168},{48,176},{56,1... | collective-permute-start | bytes 1572872 | tf_op jit(solution)/shard_map/ppermute | solution.py:230
  90.5 22.3 %collective-permute-start.9 = (bf16[8,64,512]{2,1,0:T(8,128)(2,1)}, bf16[8,64,512]{2,1,0:T(8,128)(2,1)}, u32[]{:S(2)}, u32[]{:S(2)}) collective-permute-start(bf16[8,64,512]{2,1,0:T(8,128)(2,1)} %get-tuple-element.19.refs_0_), channel_id=1, source_target_pairs={{0,384},{8,392},{16,400},{24,408},{32,416},{40,424},{48,432},{56,4... | collective-permute-start | bytes 1572872 | tf_op jit(solution)/shard_map/ppermute | solution.py:230
  97.1 21.2 %collective-permute-start.11 = (bf16[8,64,512]{2,1,0:T(8,128)(2,1)}, bf16[8,64,512]{2,1,0:T(8,128)(2,1)S(1)}, u32[]{:S(2)}, u32[]{:S(2)}) collective-permute-start(bf16[8,64,512]{2,1,0:T(8,128)(2,1)} %collective-permute-done.7.refs_2_), channel_id=1, source_target_pairs={{0,128},{8,136},{16,144},{24,152},{32,160},{40,168},{48,176},{56,1... | collective-permute-start | bytes 1572872 | tf_op jit(solution)/shard_map/ppermute | solution.py:230
  101.7 17.6 %collective-permute-start.12 = (bf16[8,64,512]{2,1,0:T(8,128)(2,1)}, bf16[8,64,512]{2,1,0:T(8,128)(2,1)S(1)}, u32[]{:S(2)}, u32[]{:S(2)}) collective-permute-start(bf16[8,64,512]{2,1,0:T(8,128)(2,1)} %collective-permute-done.10.refs_5_), channel_id=1, source_target_pairs={{0,384},{8,392},{16,400},{24,408},{32,416},{40,424},{48,432},{56,4... | collective-permute-start | bytes 1572872 | tf_op jit(solution)/shard_map/ppermute | solution.py:230
  112.9 1.0 copy-start.3
  113.9 1.0 copy-start.4
  120.1 3.8 %collective-permute-start.13 = (bf16[256,1024]{1,0:T(8,128)(2,1)S(1)}, bf16[256,1024]{1,0:T(8,128)(2,1)S(1)}, u32[]{:S(2)}, u32[]{:S(2)}) collective-permute-start(bf16[256,1024]{1,0:T(8,128)(2,1)S(1)} %get-tuple-element.22), channel_id=1, source_target_pairs={{0,1},{1,0},{2,3},{3,2},{4,5},{5,4},{6,7},{7,6},{8,9},{9,8},{10,11... | collective-permute-start | bytes 1572872 | tf_op jit(solution)/shard_map/ppermute | solution.py:287
  (3 other events, 2.3 us)

commit v5 on v4

--- a/solution.py
+++ b/solution.py
@@ -133,33 +133,31 @@
 
 
 def place_kernel(place_ref, *refs):
-    *stacks, low_ref, high_ref, arrived = refs
+    *stacks, low_ref, high_ref = refs
     z = place_ref[0]
     even = 1 - 2 * (z % 2)
     half = NZ // 2
-    waits = []
     for stack, shift in zip(stacks, (0, 1, -1, 2 * even)):
         for index, turn in enumerate((0, 1, -1, 2)):
             owner = (z - shift - NL * turn + 2 * NZ) % NZ
-            semaphore = arrived.at[len(waits)]
-            to_low = pltpu.make_async_copy(stack.at[index], low_ref.at[owner % half], semaphore)
-            to_high = pltpu.make_async_copy(stack.at[index], high_ref.at[owner % half], semaphore)
-            pl.when(owner < half)(to_low.start)
-            pl.when(owner >= half)(to_high.start)
-            waits.append(to_low)
-    for copy in waits:
-        copy.wait()
+
+            @pl.when(owner < half)
+            def _():
+                low_ref[owner % half] = stack[index]
+
+            @pl.when(owner >= half)
+            def _():
+                high_ref[owner % half] = stack[index]
 
 
 def placed(z, stacks, cost):
     half = jax.ShapeDtypeStruct((NZ // 2, *stacks[0].shape[1:]), bf16)
     return pl.pallas_call(
         place_kernel,
-        in_specs=[pl.BlockSpec(memory_space=pltpu.SMEM)] + [pl.BlockSpec(memory_space=pl.ANY)] * len(stacks),
+        in_specs=[pl.BlockSpec(memory_space=pltpu.SMEM)] + [VMEM] * len(stacks),
         out_specs=[VMEM, VMEM],
         out_shape=[half, half],
-        scratch_shapes=[pltpu.SemaphoreType.DMA((NZ,))],
-        compiler_params=pltpu.CompilerParams(vmem_limit_bytes=56 << 20),
+        compiler_params=pltpu.CompilerParams(vmem_limit_bytes=32 << 20),
         cost_estimate=pl.CostEstimate(flops=cost, bytes_accessed=2 << 20, transcendentals=0),
     )(z, *stacks)
 

time: 139 us -> 137 us (0.986)
  local copies, waits for them, and re-layouts: 4.56 us -> 1.59 us
  waiting for transfers between devices: 21.5 us -> 23.5 us
    unnamed x20 -> x8, local copies, waits for them, and re-layouts: 2.97 us -> 0.03 us
    ppermute x6, waiting for transfers between devices: 14.9 us -> 16.9 us  [along_y(): return lax.ppermute(block, 'seq', pairs)]
where the time goes in v5:
time: 137 us; the launch traced here: 136 us
  starting transfers between devices  85.5 us (62%)
  waiting for transfers between devices  23.5 us (17%)
  blocking collectives  13.2 us (10%)
  Pallas kernels  12.2 us (9%)
  local copies, waits for them, and re-layouts  1.59 us (1%)
    ppermute x6, starting transfers between devices, along_z(): return lax.ppermute(block, 'seq', pairs)  32.1 us
    all_to_all x1, starting transfers between devices, body(): lax.all_to_all(memory.reshape(blocks, -1, DH), 'seq', 0, 0, tiled=True)  19.1 us
    ppermute x6, starting transfers between devices, along_y(): return lax.ppermute(block, 'seq', pairs)  18.9 us
    ppermute x6, waiting for transfers between devices, along_y(): return lax.ppermute(block, 'seq', pairs)  16.9 us
    all_to_all x1, blocking collectives, body(): lax.all_to_all(summed.reshape(NX, rows // 8, -1), 'head', 0, 0, tiled=Tru...  13.2 us
    all_to_all x1, starting transfers between devices, body(): prior = lax.all_to_all(sums, 'seq', 0, 0, tiled=True).reshape(width, DH)  5.51 us
    pallas_call x3, Pallas kernels, placed_call(): pl.pallas_call(kernel, in_specs=[pl.BlockSpec(memory_space=pltpu.SMEM)] +...  4.89 us
    all_to_all x1, waiting for transfers between devices, body(): prior = lax.all_to_all(sums, 'seq', 0, 0, tiled=True).reshape(width, DH)  4.68 us
  transfers between devices with their start and end apart: 17, of which 6 were waited for; matrix products, arithmetic and copies ran while one was open for 1% of the time, Pallas kernels for 8%

profile of v5, /device:TPU:24, one launch (start us, length us, event | category | flops | bytes accessed | tf_op | source)
XLA Modules:
  0.0 136.2 jit_solution(3795550366985799041)
XLA Ops:
  0.0 4.3 %collective-permute-start = (bf16[64,512]{1,0:T(8,128)(2,1)}, bf16[64,512]{1,0:T(8,128)(2,1)S(1)}, u32[]{:S(2)}, u32[]{:S(2)}) collective-permute-start(bf16[64,512]{1,0:T(8,128)(2,1)} %bitcast.12), channel_id=1, source_target_pairs={{0,0},{1,1},{2,128},{3,129},{4,256},{5,257},{6,384},{7,385},{8,8},... | collective-permute-start | bytes 196616 | tf_op jit(solution)/shard_map/ppermute | solution.py:218
  4.3 2.8 %shard_map.55 = (bf16[512,512]{1,0:T(8,128)(2,1)}, bf16[512,128]{1,0:T(8,128)(2,1)}) custom-call(bf16[512,512]{1,0:T(8,128)(2,1)} %keys_ref.1, bf16[512,512]{1,0:T(8,128)(2,1)} %values_ref.3), custom_call_target="tpu_custom_call" | custom-call | flops 67108864 | bytes 2097152 | tf_op jit(solution)/shard_map/pallas_call | solution.py:67
  7.2 19.1 %all-to-all-start = ((bf16[64,8,128]{2,1,0:T(8,128)(2,1)}), bf16[64,8,128]{2,1,0:T(8,128)(2,1)S(1)}, u32[]{:S(2)}, u32[]{:S(2)}) async-start(bf16[64,8,128]{2,1,0:T(8,128)(2,1)} %bitcast.11), calls=%async_computation | async-start | bytes 262144 | tf_op jit(solution)/shard_map/all_to_all | solution.py:247
  26.3 7.3 %collective-permute-start.1 = (bf16[64,512]{1,0:T(8,128)(2,1)S(1)}, bf16[64,512]{1,0:T(8,128)(2,1)S(1)}, u32[]{:S(2)}, u32[]{:S(2)}) collective-permute-start(bf16[64,512]{1,0:T(8,128)(2,1)S(1)} %shard_map.59.refs_0_), channel_id=1, source_target_pairs={{0,32},{8,40},{16,48},{24,56},{32,64},{40,72},{48,80},{56,88},{64,... | collective-permute-start | bytes 196616 | tf_op jit(solution)/shard_map/ppermute | solution.py:223
  33.6 2.4 %collective-permute-start.2 = (bf16[64,512]{1,0:T(8,128)(2,1)S(1)}, bf16[64,512]{1,0:T(8,128)(2,1)S(1)}, u32[]{:S(2)}, u32[]{:S(2)}) collective-permute-start(bf16[64,512]{1,0:T(8,128)(2,1)S(1)} %shard_map.59.refs_0_), channel_id=1, source_target_pairs={{0,96},{8,104},{16,112},{24,120},{32,0},{40,8},{48,16},{56,24},{64... | collective-permute-start | bytes 196616 | tf_op jit(solution)/shard_map/ppermute | solution.py:223
  36.1 12.1 %collective-permute-start.3 = (bf16[64,512]{1,0:T(8,128)(2,1)S(1)}, bf16[64,512]{1,0:T(8,128)(2,1)S(1)}, u32[]{:S(2)}, u32[]{:S(2)}) collective-permute-start(bf16[64,512]{1,0:T(8,128)(2,1)S(1)} %shard_map.59.refs_0_), channel_id=1, source_target_pairs={{0,64},{8,72},{16,80},{24,88},{32,96},{40,104},{48,112},{56,120},{... | collective-permute-start | bytes 196616 | tf_op jit(solution)/shard_map/ppermute | solution.py:223
  49.0 5.5 %all-to-all-start.1 = ((bf16[64,8,128]{2,1,0:T(8,128)(2,1)}), bf16[64,8,128]{2,1,0:T(8,128)(2,1)S(1)}, u32[]{:S(2)}, u32[]{:S(2)}) async-start(bf16[64,8,128]{2,1,0:T(8,128)(2,1)} %shard_map.56), calls=%async_computation.1 | async-start | bytes 262144 | tf_op jit(solution)/shard_map/all_to_all | solution.py:251
  54.6 3.5 %collective-permute-start.4 = (bf16[4,64,512]{2,1,0:T(8,128)(2,1)S(1)}, bf16[4,64,512]{2,1,0:T(8,128)(2,1)S(1)}, u32[]{:S(2)}, u32[]{:S(2)}) collective-permute-start(bf16[4,64,512]{2,1,0:T(8,128)(2,1)S(1)} %shard_map.60.refs_0_), channel_id=1, source_target_pairs={{0,8},{8,16},{16,24},{24,32},{32,40},{40,48},{48,56},{56,64},{64,7... | collective-permute-start | bytes 786440 | tf_op jit(solution)/shard_map/ppermute | solution.py:223
  58.1 4.0 %collective-permute-start.5 = (bf16[4,64,512]{2,1,0:T(8,128)(2,1)S(1)}, bf16[4,64,512]{2,1,0:T(8,128)(2,1)S(1)}, u32[]{:S(2)}, u32[]{:S(2)}) collective-permute-start(bf16[4,64,512]{2,1,0:T(8,128)(2,1)S(1)} %shard_map.60.refs_0_), channel_id=1, source_target_pairs={{0,120},{8,0},{16,8},{24,16},{32,24},{40,32},{48,40},{56,48},{64,5... | collective-permute-start | bytes 786440 | tf_op jit(solution)/shard_map/ppermute | solution.py:223
  62.1 2.8 %collective-permute-start.6 = (bf16[4,64,512]{2,1,0:T(8,128)(2,1)S(1)}, bf16[4,64,512]{2,1,0:T(8,128)(2,1)S(1)}, u32[]{:S(2)}, u32[]{:S(2)}) collective-permute-start(bf16[4,64,512]{2,1,0:T(8,128)(2,1)S(1)} %shard_map.60.refs_0_), channel_id=1, source_target_pairs={{0,16},{8,120},{16,32},{24,8},{32,48},{40,24},{48,64},{56,40},{64,... | collective-permute-start | bytes 786440 | tf_op jit(solution)/shard_map/ppermute | solution.py:223
  64.9 4.7 %all-to-all-done.1 = bf16[64,8,128]{2,1,0:T(8,128)(2,1)S(1)} async-done(((bf16[64,8,128]{2,1,0:T(8,128)(2,1)}), bf16[64,8,128]{2,1,0:T(8,128)(2,1)S(1)}, u32[]{:S(2)}, u32[]{:S(2)}) %all-to-all-start.1) | async-done | bytes 131104 | tf_op jit(solution)/shard_map/all_to_all | solution.py:251
  73.1 3.6 %all-to-all-start.2 = ((bf16[4,2,4,64,512]{4,3,2,1,0:T(8,128)(2,1)}), bf16[4,2,4,64,512]{4,3,2,1,0:T(8,128)(2,1)S(1)}, u32[]{:S(2)}, u32[]{:S(2)}) async-start(bf16[4,2,4,64,512]{4,3,2,1,0:T(8,128)(2,1)} %broadcast_in_dim.2), calls=%async_computation.2 | async-start | bytes 4194304 | tf_op jit(solution)/shard_map/all_to_all | solution.py:271
  78.1 3.4 %collective-permute-start.7 = (bf16[8,64,512]{2,1,0:T(8,128)(2,1)}, bf16[8,64,512]{2,1,0:T(8,128)(2,1)}, u32[]{:S(2)}, u32[]{:S(2)}) collective-permute-start(bf16[8,64,512]{2,1,0:T(8,128)(2,1)} %get-tuple-element.19.refs_0_), channel_id=1, source_target_pairs={{0,128},{8,136},{16,144},{24,152},{32,160},{40,168},{48,176},{56,1... | collective-permute-start | bytes 1572872 | tf_op jit(solution)/shard_map/ppermute | solution.py:228
  81.5 2.5 %collective-permute-start.10 = (bf16[8,64,512]{2,1,0:T(8,128)(2,1)}, bf16[8,64,512]{2,1,0:T(8,128)(2,1)}, u32[]{:S(2)}, u32[]{:S(2)}) collective-permute-start(bf16[8,64,512]{2,1,0:T(8,128)(2,1)} %get-tuple-element.20.refs_1_), channel_id=1, source_target_pairs={{0,384},{8,392},{16,400},{24,408},{32,416},{40,424},{48,432},{56,4... | collective-permute-start | bytes 1572872 | tf_op jit(solution)/shard_map/ppermute | solution.py:228
  83.9 4.6 %collective-permute-start.8 = (bf16[8,64,512]{2,1,0:T(8,128)(2,1)}, bf16[8,64,512]{2,1,0:T(8,128)(2,1)}, u32[]{:S(2)}, u32[]{:S(2)}) collective-permute-start(bf16[8,64,512]{2,1,0:T(8,128)(2,1)} %get-tuple-element.20.refs_1_), channel_id=1, source_target_pairs={{0,128},{8,136},{16,144},{24,152},{32,160},{40,168},{48,176},{56,1... | collective-permute-start | bytes 1572872 | tf_op jit(solution)/shard_map/ppermute | solution.py:228
  88.6 1.9 %collective-permute-start.9 = (bf16[8,64,512]{2,1,0:T(8,128)(2,1)}, bf16[8,64,512]{2,1,0:T(8,128)(2,1)}, u32[]{:S(2)}, u32[]{:S(2)}) collective-permute-start(bf16[8,64,512]{2,1,0:T(8,128)(2,1)} %get-tuple-element.19.refs_0_), channel_id=1, source_target_pairs={{0,384},{8,392},{16,400},{24,408},{32,416},{40,424},{48,432},{56,4... | collective-permute-start | bytes 1572872 | tf_op jit(solution)/shard_map/ppermute | solution.py:228
  90.5 4.7 %collective-permute-done.7.refs_2_ = bf16[8,64,512]{2,1,0:T(8,128)(2,1)} collective-permute-done((bf16[8,64,512]{2,1,0:T(8,128)(2,1)}, bf16[8,64,512]{2,1,0:T(8,128)(2,1)}, u32[]{:S(2)}, u32[]{:S(2)}) %collective-permute-start.7) | collective-permute-done | bytes 524320 | tf_op jit(solution)/shard_map/ppermute | solution.py:228
  95.2 4.6 %collective-permute-start.11 = (bf16[8,64,512]{2,1,0:T(8,128)(2,1)}, bf16[8,64,512]{2,1,0:T(8,128)(2,1)S(1)}, u32[]{:S(2)}, u32[]{:S(2)}) collective-permute-start(bf16[8,64,512]{2,1,0:T(8,128)(2,1)} %collective-permute-done.7.refs_2_), channel_id=1, source_target_pairs={{0,128},{8,136},{16,144},{24,152},{32,160},{40,168},{48,176},{56,1... | collective-permute-start | bytes 1572872 | tf_op jit(solution)/shard_map/ppermute | solution.py:228
  101.7 4.7 %collective-permute-done.8.refs_3_ = bf16[8,64,512]{2,1,0:T(8,128)(2,1)} collective-permute-done((bf16[8,64,512]{2,1,0:T(8,128)(2,1)}, bf16[8,64,512]{2,1,0:T(8,128)(2,1)}, u32[]{:S(2)}, u32[]{:S(2)}) %collective-permute-start.8) | collective-permute-done | bytes 524320 | tf_op jit(solution)/shard_map/ppermute | solution.py:228
  106.4 4.6 %collective-permute-done.9.refs_4_ = bf16[8,64,512]{2,1,0:T(8,128)(2,1)} collective-permute-done((bf16[8,64,512]{2,1,0:T(8,128)(2,1)}, bf16[8,64,512]{2,1,0:T(8,128)(2,1)}, u32[]{:S(2)}, u32[]{:S(2)}) %collective-permute-start.9) | collective-permute-done | bytes 524320 | tf_op jit(solution)/shard_map/ppermute | solution.py:228
  111.0 3.6 %shard_map.62.total_ref = f32[512,1024]{1,0:T(8,128)S(1)} custom-call(s32[1]{0:T(128)} %bitcast.place_ref, bf16[4,2,4,64,512]{4,3,2,1,0:T(8,128)(2,1)S(1)} %all-to-all-done.2.tokens_ref, bf16[8,64,512]{2,1,0:T(8,128)(2,1)} %get-tuple-element.19.refs_0_, bf16[8,64,512]{2,1,0:T(8,128)(2,1)} %get-tuple-element.20.refs_1_, ...), custom_call_target="tpu_custom_call" | custom-call | flops 8589934592 | bytes 4194304 | tf_op jit(solution)/shard_map/pallas_call | solution.py:29
  114.7 2.9 %collective-permute-done.12.second_ref = bf16[8,64,512]{2,1,0:T(8,128)(2,1)S(1)} collective-permute-done((bf16[8,64,512]{2,1,0:T(8,128)(2,1)}, bf16[8,64,512]{2,1,0:T(8,128)(2,1)S(1)}, u32[]{:S(2)}, u32[]{:S(2)}) %collective-permute-start.12) | collective-permute-done | bytes 524320 | tf_op jit(solution)/shard_map/ppermute | solution.py:228
  118.3 1.9 %collective-permute-start.13 = (bf16[256,1024]{1,0:T(8,128)(2,1)S(1)}, bf16[256,1024]{1,0:T(8,128)(2,1)S(1)}, u32[]{:S(2)}, u32[]{:S(2)}) collective-permute-start(bf16[256,1024]{1,0:T(8,128)(2,1)S(1)} %get-tuple-element.22), channel_id=1, source_target_pairs={{0,1},{1,0},{2,3},{3,2},{4,5},{5,4},{6,7},{7,6},{8,9},{9,8},{10,11... | collective-permute-start | bytes 1572872 | tf_op jit(solution)/shard_map/ppermute | solution.py:285
  122.2 13.2 %all_to_all.20.parts_ref = bf16[4,64,1024]{2,1,0:T(8,128)(2,1)S(1)} all-to-all(bf16[4,64,1024]{2,1,0:T(8,128)(2,1)S(1)} %bitcast.8), channel_id=1, replica_groups={{0,2,4,6},{1,3,5,7},{8,10,12,14},{9,11,13,15},{16,18,20,22},{17,19,21,2..., dimensions={0} | all-to-all | bytes 1048576 | tf_op jit(solution)/shard_map/all_to_all | solution.py:287
  (31 shorter events, 11.1 us)
Async XLA Ops:
  0.0 26.3 %collective-permute-start = (bf16[64,512]{1,0:T(8,128)(2,1)}, bf16[64,512]{1,0:T(8,128)(2,1)S(1)}, u32[]{:S(2)}, u32[]{:S(2)}) collective-permute-start(bf16[64,512]{1,0:T(8,128)(2,1)} %bitcast.12), channel_id=1, source_target_pairs={{0,0},{1,1},{2,128},{3,129},{4,256},{5,257},{6,384},{7,385},{8,8},... | collective-permute-start | bytes 196616 | tf_op jit(solution)/shard_map/ppermute | solution.py:218
  7.2 41.1 %all-to-all-start = ((bf16[64,8,128]{2,1,0:T(8,128)(2,1)}), bf16[64,8,128]{2,1,0:T(8,128)(2,1)S(1)}, u32[]{:S(2)}, u32[]{:S(2)}) async-start(bf16[64,8,128]{2,1,0:T(8,128)(2,1)} %bitcast.11), calls=%async_computation | async-start | bytes 262144 | tf_op jit(solution)/shard_map/all_to_all | solution.py:247
  26.3 28.2 %collective-permute-start.1 = (bf16[64,512]{1,0:T(8,128)(2,1)S(1)}, bf16[64,512]{1,0:T(8,128)(2,1)S(1)}, u32[]{:S(2)}, u32[]{:S(2)}) collective-permute-start(bf16[64,512]{1,0:T(8,128)(2,1)S(1)} %shard_map.59.refs_0_), channel_id=1, source_target_pairs={{0,32},{8,40},{16,48},{24,56},{32,64},{40,72},{48,80},{56,88},{64,... | collective-permute-start | bytes 196616 | tf_op jit(solution)/shard_map/ppermute | solution.py:223
  33.6 20.9 %collective-permute-start.2 = (bf16[64,512]{1,0:T(8,128)(2,1)S(1)}, bf16[64,512]{1,0:T(8,128)(2,1)S(1)}, u32[]{:S(2)}, u32[]{:S(2)}) collective-permute-start(bf16[64,512]{1,0:T(8,128)(2,1)S(1)} %shard_map.59.refs_0_), channel_id=1, source_target_pairs={{0,96},{8,104},{16,112},{24,120},{32,0},{40,8},{48,16},{56,24},{64... | collective-permute-start | bytes 196616 | tf_op jit(solution)/shard_map/ppermute | solution.py:223
  36.1 18.5 %collective-permute-start.3 = (bf16[64,512]{1,0:T(8,128)(2,1)S(1)}, bf16[64,512]{1,0:T(8,128)(2,1)S(1)}, u32[]{:S(2)}, u32[]{:S(2)}) collective-permute-start(bf16[64,512]{1,0:T(8,128)(2,1)S(1)} %shard_map.59.refs_0_), channel_id=1, source_target_pairs={{0,64},{8,72},{16,80},{24,88},{32,96},{40,104},{48,112},{56,120},{... | collective-permute-start | bytes 196616 | tf_op jit(solution)/shard_map/ppermute | solution.py:223
  49.0 20.6 %all-to-all-start.1 = ((bf16[64,8,128]{2,1,0:T(8,128)(2,1)}), bf16[64,8,128]{2,1,0:T(8,128)(2,1)S(1)}, u32[]{:S(2)}, u32[]{:S(2)}) async-start(bf16[64,8,128]{2,1,0:T(8,128)(2,1)} %shard_map.56), calls=%async_computation.1 | async-start | bytes 262144 | tf_op jit(solution)/shard_map/all_to_all | solution.py:251
  54.5 15.1 %copy-start = (bf16[512,512]{1,0:T(8,128)(2,1)S(1)}, bf16[512,512]{1,0:T(8,128)(2,1)}, u32[]{:S(2)}) copy-start(bf16[512,512]{1,0:T(8,128)(2,1)} %values_ref.3) | copy-start | bytes 1572868
  54.5 15.1 %copy-start.1 = (bf16[512,512]{1,0:T(8,128)(2,1)S(1)}, bf16[512,512]{1,0:T(8,128)(2,1)}, u32[]{:S(2)}) copy-start(bf16[512,512]{1,0:T(8,128)(2,1)} %queries_ref) | copy-start | bytes 1572868
  54.5 15.0 %copy-start.2 = (bf16[512,512]{1,0:T(8,128)(2,1)S(1)}, bf16[512,512]{1,0:T(8,128)(2,1)}, u32[]{:S(2)}) copy-start(bf16[512,512]{1,0:T(8,128)(2,1)} %get-tuple-element.16.key_ref) | copy-start | bytes 1572868
  54.5 16.5 %copy-start.3 = (f32[512]{0:T(512)S(1)}, f32[512]{0:T(512)}, u32[]{:S(2)}) copy-start(f32[512]{0:T(512)} %param.9) | copy-start | bytes 6148
  54.6 22.2 %collective-permute-start.4 = (bf16[4,64,512]{2,1,0:T(8,128)(2,1)S(1)}, bf16[4,64,512]{2,1,0:T(8,128)(2,1)S(1)}, u32[]{:S(2)}, u32[]{:S(2)}) collective-permute-start(bf16[4,64,512]{2,1,0:T(8,128)(2,1)S(1)} %shard_map.60.refs_0_), channel_id=1, source_target_pairs={{0,8},{8,16},{16,24},{24,32},{32,40},{40,48},{48,56},{56,64},{64,7... | collective-permute-start | bytes 786440 | tf_op jit(solution)/shard_map/ppermute | solution.py:223
  58.1 18.7 %collective-permute-start.5 = (bf16[4,64,512]{2,1,0:T(8,128)(2,1)S(1)}, bf16[4,64,512]{2,1,0:T(8,128)(2,1)S(1)}, u32[]{:S(2)}, u32[]{:S(2)}) collective-permute-start(bf16[4,64,512]{2,1,0:T(8,128)(2,1)S(1)} %shard_map.60.refs_0_), channel_id=1, source_target_pairs={{0,120},{8,0},{16,8},{24,16},{32,24},{40,32},{48,40},{56,48},{64,5... | collective-permute-start | bytes 786440 | tf_op jit(solution)/shard_map/ppermute | solution.py:223
  62.1 14.7 %collective-permute-start.6 = (bf16[4,64,512]{2,1,0:T(8,128)(2,1)S(1)}, bf16[4,64,512]{2,1,0:T(8,128)(2,1)S(1)}, u32[]{:S(2)}, u32[]{:S(2)}) collective-permute-start(bf16[4,64,512]{2,1,0:T(8,128)(2,1)S(1)} %shard_map.60.refs_0_), channel_id=1, source_target_pairs={{0,16},{8,120},{16,32},{24,8},{32,48},{40,24},{48,64},{56,40},{64,... | collective-permute-start | bytes 786440 | tf_op jit(solution)/shard_map/ppermute | solution.py:223
  73.1 37.9 %all-to-all-start.2 = ((bf16[4,2,4,64,512]{4,3,2,1,0:T(8,128)(2,1)}), bf16[4,2,4,64,512]{4,3,2,1,0:T(8,128)(2,1)S(1)}, u32[]{:S(2)}, u32[]{:S(2)}) async-start(bf16[4,2,4,64,512]{4,3,2,1,0:T(8,128)(2,1)} %broadcast_in_dim.2), calls=%async_computation.2 | async-start | bytes 4194304 | tf_op jit(solution)/shard_map/all_to_all | solution.py:271
  78.1 17.1 %collective-permute-start.7 = (bf16[8,64,512]{2,1,0:T(8,128)(2,1)}, bf16[8,64,512]{2,1,0:T(8,128)(2,1)}, u32[]{:S(2)}, u32[]{:S(2)}) collective-permute-start(bf16[8,64,512]{2,1,0:T(8,128)(2,1)} %get-tuple-element.19.refs_0_), channel_id=1, source_target_pairs={{0,128},{8,136},{16,144},{24,152},{32,160},{40,168},{48,176},{56,1... | collective-permute-start | bytes 1572872 | tf_op jit(solution)/shard_map/ppermute | solution.py:228
  81.5 18.3 %collective-permute-start.10 = (bf16[8,64,512]{2,1,0:T(8,128)(2,1)}, bf16[8,64,512]{2,1,0:T(8,128)(2,1)}, u32[]{:S(2)}, u32[]{:S(2)}) collective-permute-start(bf16[8,64,512]{2,1,0:T(8,128)(2,1)} %get-tuple-element.20.refs_1_), channel_id=1, source_target_pairs={{0,384},{8,392},{16,400},{24,408},{32,416},{40,424},{48,432},{56,4... | collective-permute-start | bytes 1572872 | tf_op jit(solution)/shard_map/ppermute | solution.py:228
  83.9 22.4 %collective-permute-start.8 = (bf16[8,64,512]{2,1,0:T(8,128)(2,1)}, bf16[8,64,512]{2,1,0:T(8,128)(2,1)}, u32[]{:S(2)}, u32[]{:S(2)}) collective-permute-start(bf16[8,64,512]{2,1,0:T(8,128)(2,1)} %get-tuple-element.20.refs_1_), channel_id=1, source_target_pairs={{0,128},{8,136},{16,144},{24,152},{32,160},{40,168},{48,176},{56,1... | collective-permute-start | bytes 1572872 | tf_op jit(solution)/shard_map/ppermute | solution.py:228
  88.6 22.4 %collective-permute-start.9 = (bf16[8,64,512]{2,1,0:T(8,128)(2,1)}, bf16[8,64,512]{2,1,0:T(8,128)(2,1)}, u32[]{:S(2)}, u32[]{:S(2)}) collective-permute-start(bf16[8,64,512]{2,1,0:T(8,128)(2,1)} %get-tuple-element.19.refs_0_), channel_id=1, source_target_pairs={{0,384},{8,392},{16,400},{24,408},{32,416},{40,424},{48,432},{56,4... | collective-permute-start | bytes 1572872 | tf_op jit(solution)/shard_map/ppermute | solution.py:228
  95.2 19.5 %collective-permute-start.11 = (bf16[8,64,512]{2,1,0:T(8,128)(2,1)}, bf16[8,64,512]{2,1,0:T(8,128)(2,1)S(1)}, u32[]{:S(2)}, u32[]{:S(2)}) collective-permute-start(bf16[8,64,512]{2,1,0:T(8,128)(2,1)} %collective-permute-done.7.refs_2_), channel_id=1, source_target_pairs={{0,128},{8,136},{16,144},{24,152},{32,160},{40,168},{48,176},{56,1... | collective-permute-start | bytes 1572872 | tf_op jit(solution)/shard_map/ppermute | solution.py:228
  99.8 17.8 %collective-permute-start.12 = (bf16[8,64,512]{2,1,0:T(8,128)(2,1)}, bf16[8,64,512]{2,1,0:T(8,128)(2,1)S(1)}, u32[]{:S(2)}, u32[]{:S(2)}) collective-permute-start(bf16[8,64,512]{2,1,0:T(8,128)(2,1)} %collective-permute-done.10.refs_5_), channel_id=1, source_target_pairs={{0,384},{8,392},{16,400},{24,408},{32,416},{40,424},{48,432},{56,4... | collective-permute-start | bytes 1572872 | tf_op jit(solution)/shard_map/ppermute | solution.py:228
  118.3 3.8 %collective-permute-start.13 = (bf16[256,1024]{1,0:T(8,128)(2,1)S(1)}, bf16[256,1024]{1,0:T(8,128)(2,1)S(1)}, u32[]{:S(2)}, u32[]{:S(2)}) collective-permute-start(bf16[256,1024]{1,0:T(8,128)(2,1)S(1)} %get-tuple-element.22), channel_id=1, source_target_pairs={{0,1},{1,0},{2,3},{3,2},{4,5},{5,4},{6,7},{7,6},{8,9},{9,8},{10,11... | collective-permute-start | bytes 1572872 | tf_op jit(solution)/shard_map/ppermute | solution.py:285

commit v6 on v4

--- a/solution.py
+++ b/solution.py
@@ -155,11 +155,11 @@
     half = jax.ShapeDtypeStruct((NZ // 2, *stacks[0].shape[1:]), bf16)
     return pl.pallas_call(
         place_kernel,
-        in_specs=[pl.BlockSpec(memory_space=pltpu.SMEM)] + [pl.BlockSpec(memory_space=pl.ANY)] * len(stacks),
-        out_specs=[VMEM, VMEM],
+        in_specs=[pl.BlockSpec(memory_space=pltpu.SMEM)] + [VMEM] * len(stacks),
+        out_specs=[pl.BlockSpec(memory_space=pl.ANY)] * 2,
         out_shape=[half, half],
         scratch_shapes=[pltpu.SemaphoreType.DMA((NZ,))],
-        compiler_params=pltpu.CompilerParams(vmem_limit_bytes=56 << 20),
+        compiler_params=pltpu.CompilerParams(vmem_limit_bytes=32 << 20),
         cost_estimate=pl.CostEstimate(flops=cost, bytes_accessed=2 << 20, transcendentals=0),
     )(z, *stacks)
 

time: 139 us -> 137 us (0.986)
  local copies, waits for them, and re-layouts: 4.56 us -> 1.59 us
  waiting for transfers between devices: 21.5 us -> 23.5 us
    unnamed x20 -> x8, local copies, waits for them, and re-layouts: 2.97 us -> 0.03 us
    ppermute x6, waiting for transfers between devices: 14.9 us -> 16.9 us  [along_y(): return lax.ppermute(block, 'seq', pairs)]
where the time goes in v6:
time: 137 us; the launch traced here: 136 us
  starting transfers between devices  85.5 us (62%)
  waiting for transfers between devices  23.5 us (17%)
  blocking collectives  13.2 us (10%)
  Pallas kernels  12 us (9%)
  local copies, waits for them, and re-layouts  1.59 us (1%)
    ppermute x6, starting transfers between devices, along_z(): return lax.ppermute(block, 'seq', pairs)  32.1 us
    all_to_all x1, starting transfers between devices, body(): lax.all_to_all(memory.reshape(blocks, -1, DH), 'seq', 0, 0, tiled=True)  19.1 us
    ppermute x6, starting transfers between devices, along_y(): return lax.ppermute(block, 'seq', pairs)  18.9 us
    ppermute x6, waiting for transfers between devices, along_y(): return lax.ppermute(block, 'seq', pairs)  16.9 us
    all_to_all x1, blocking collectives, body(): lax.all_to_all(summed.reshape(NX, rows // 8, -1), 'head', 0, 0, tiled=Tru...  13.2 us
    all_to_all x1, starting transfers between devices, body(): prior = lax.all_to_all(sums, 'seq', 0, 0, tiled=True).reshape(width, DH)  5.51 us
    pallas_call x3, Pallas kernels, placed_call(): pl.pallas_call(kernel, in_specs=[pl.BlockSpec(memory_space=pltpu.SMEM)] +...  4.89 us
    all_to_all x1, waiting for transfers between devices, body(): prior = lax.all_to_all(sums, 'seq', 0, 0, tiled=True).reshape(width, DH)  4.68 us
  transfers between devices with their start and end apart: 17, of which 6 were waited for; matrix products, arithmetic and copies ran while one was open for 1% of the time, Pallas kernels for 8%

profile of v6, /device:TPU:24, one launch (start us, length us, event | category | flops | bytes accessed | tf_op | source)
XLA Modules:
  0.0 136.0 jit_solution(9222112704468704027)
XLA Ops:
  0.0 4.3 %collective-permute-start = (bf16[64,512]{1,0:T(8,128)(2,1)}, bf16[64,512]{1,0:T(8,128)(2,1)S(1)}, u32[]{:S(2)}, u32[]{:S(2)}) collective-permute-start(bf16[64,512]{1,0:T(8,128)(2,1)} %bitcast.12), channel_id=1, source_target_pairs={{0,0},{1,1},{2,128},{3,129},{4,256},{5,257},{6,384},{7,385},{8,8},... | collective-permute-start | bytes 196616 | tf_op jit(solution)/shard_map/ppermute | solution.py:220
  4.3 2.8 %shard_map.55 = (bf16[512,512]{1,0:T(8,128)(2,1)}, bf16[512,128]{1,0:T(8,128)(2,1)}) custom-call(bf16[512,512]{1,0:T(8,128)(2,1)} %keys_ref.1, bf16[512,512]{1,0:T(8,128)(2,1)} %values_ref.3), custom_call_target="tpu_custom_call" | custom-call | flops 67108864 | bytes 2097152 | tf_op jit(solution)/shard_map/pallas_call | solution.py:67
  7.2 19.1 %all-to-all-start = ((bf16[64,8,128]{2,1,0:T(8,128)(2,1)}), bf16[64,8,128]{2,1,0:T(8,128)(2,1)S(1)}, u32[]{:S(2)}, u32[]{:S(2)}) async-start(bf16[64,8,128]{2,1,0:T(8,128)(2,1)} %bitcast.11), calls=%async_computation | async-start | bytes 262144 | tf_op jit(solution)/shard_map/all_to_all | solution.py:249
  26.3 7.3 %collective-permute-start.1 = (bf16[64,512]{1,0:T(8,128)(2,1)S(1)}, bf16[64,512]{1,0:T(8,128)(2,1)S(1)}, u32[]{:S(2)}, u32[]{:S(2)}) collective-permute-start(bf16[64,512]{1,0:T(8,128)(2,1)S(1)} %shard_map.59.refs_0_), channel_id=1, source_target_pairs={{0,32},{8,40},{16,48},{24,56},{32,64},{40,72},{48,80},{56,88},{64,... | collective-permute-start | bytes 196616 | tf_op jit(solution)/shard_map/ppermute | solution.py:225
  33.6 2.4 %collective-permute-start.2 = (bf16[64,512]{1,0:T(8,128)(2,1)S(1)}, bf16[64,512]{1,0:T(8,128)(2,1)S(1)}, u32[]{:S(2)}, u32[]{:S(2)}) collective-permute-start(bf16[64,512]{1,0:T(8,128)(2,1)S(1)} %shard_map.59.refs_0_), channel_id=1, source_target_pairs={{0,96},{8,104},{16,112},{24,120},{32,0},{40,8},{48,16},{56,24},{64... | collective-permute-start | bytes 196616 | tf_op jit(solution)/shard_map/ppermute | solution.py:225
  36.1 12.1 %collective-permute-start.3 = (bf16[64,512]{1,0:T(8,128)(2,1)S(1)}, bf16[64,512]{1,0:T(8,128)(2,1)S(1)}, u32[]{:S(2)}, u32[]{:S(2)}) collective-permute-start(bf16[64,512]{1,0:T(8,128)(2,1)S(1)} %shard_map.59.refs_0_), channel_id=1, source_target_pairs={{0,64},{8,72},{16,80},{24,88},{32,96},{40,104},{48,112},{56,120},{... | collective-permute-start | bytes 196616 | tf_op jit(solution)/shard_map/ppermute | solution.py:225
  49.0 5.5 %all-to-all-start.1 = ((bf16[64,8,128]{2,1,0:T(8,128)(2,1)}), bf16[64,8,128]{2,1,0:T(8,128)(2,1)S(1)}, u32[]{:S(2)}, u32[]{:S(2)}) async-start(bf16[64,8,128]{2,1,0:T(8,128)(2,1)} %shard_map.56), calls=%async_computation.1 | async-start | bytes 262144 | tf_op jit(solution)/shard_map/all_to_all | solution.py:253
  54.6 3.5 %collective-permute-start.4 = (bf16[4,64,512]{2,1,0:T(8,128)(2,1)S(1)}, bf16[4,64,512]{2,1,0:T(8,128)(2,1)S(1)}, u32[]{:S(2)}, u32[]{:S(2)}) collective-permute-start(bf16[4,64,512]{2,1,0:T(8,128)(2,1)S(1)} %shard_map.60.refs_0_), channel_id=1, source_target_pairs={{0,8},{8,16},{16,24},{24,32},{32,40},{40,48},{48,56},{56,64},{64,7... | collective-permute-start | bytes 786440 | tf_op jit(solution)/shard_map/ppermute | solution.py:225
  58.1 4.0 %collective-permute-start.5 = (bf16[4,64,512]{2,1,0:T(8,128)(2,1)S(1)}, bf16[4,64,512]{2,1,0:T(8,128)(2,1)S(1)}, u32[]{:S(2)}, u32[]{:S(2)}) collective-permute-start(bf16[4,64,512]{2,1,0:T(8,128)(2,1)S(1)} %shard_map.60.refs_0_), channel_id=1, source_target_pairs={{0,120},{8,0},{16,8},{24,16},{32,24},{40,32},{48,40},{56,48},{64,5... | collective-permute-start | bytes 786440 | tf_op jit(solution)/shard_map/ppermute | solution.py:225
  62.1 2.8 %collective-permute-start.6 = (bf16[4,64,512]{2,1,0:T(8,128)(2,1)S(1)}, bf16[4,64,512]{2,1,0:T(8,128)(2,1)S(1)}, u32[]{:S(2)}, u32[]{:S(2)}) collective-permute-start(bf16[4,64,512]{2,1,0:T(8,128)(2,1)S(1)} %shard_map.60.refs_0_), channel_id=1, source_target_pairs={{0,16},{8,120},{16,32},{24,8},{32,48},{40,24},{48,64},{56,40},{64,... | collective-permute-start | bytes 786440 | tf_op jit(solution)/shard_map/ppermute | solution.py:225
  64.9 4.7 %all-to-all-done.1 = bf16[64,8,128]{2,1,0:T(8,128)(2,1)S(1)} async-done(((bf16[64,8,128]{2,1,0:T(8,128)(2,1)}), bf16[64,8,128]{2,1,0:T(8,128)(2,1)S(1)}, u32[]{:S(2)}, u32[]{:S(2)}) %all-to-all-start.1) | async-done | bytes 131104 | tf_op jit(solution)/shard_map/all_to_all | solution.py:253
  73.1 3.6 %all-to-all-start.2 = ((bf16[4,2,4,64,512]{4,3,2,1,0:T(8,128)(2,1)}), bf16[4,2,4,64,512]{4,3,2,1,0:T(8,128)(2,1)S(1)}, u32[]{:S(2)}, u32[]{:S(2)}) async-start(bf16[4,2,4,64,512]{4,3,2,1,0:T(8,128)(2,1)} %broadcast_in_dim.2), calls=%async_computation.2 | async-start | bytes 4194304 | tf_op jit(solution)/shard_map/all_to_all | solution.py:273
  77.9 3.4 %collective-permute-start.7 = (bf16[8,64,512]{2,1,0:T(8,128)(2,1)}, bf16[8,64,512]{2,1,0:T(8,128)(2,1)}, u32[]{:S(2)}, u32[]{:S(2)}) collective-permute-start(bf16[8,64,512]{2,1,0:T(8,128)(2,1)} %get-tuple-element.19.refs_0_), channel_id=1, source_target_pairs={{0,128},{8,136},{16,144},{24,152},{32,160},{40,168},{48,176},{56,1... | collective-permute-start | bytes 1572872 | tf_op jit(solution)/shard_map/ppermute | solution.py:230
  81.3 2.5 %collective-permute-start.10 = (bf16[8,64,512]{2,1,0:T(8,128)(2,1)}, bf16[8,64,512]{2,1,0:T(8,128)(2,1)}, u32[]{:S(2)}, u32[]{:S(2)}) collective-permute-start(bf16[8,64,512]{2,1,0:T(8,128)(2,1)} %get-tuple-element.20.refs_1_), channel_id=1, source_target_pairs={{0,384},{8,392},{16,400},{24,408},{32,416},{40,424},{48,432},{56,4... | collective-permute-start | bytes 1572872 | tf_op jit(solution)/shard_map/ppermute | solution.py:230
  83.7 4.6 %collective-permute-start.8 = (bf16[8,64,512]{2,1,0:T(8,128)(2,1)}, bf16[8,64,512]{2,1,0:T(8,128)(2,1)}, u32[]{:S(2)}, u32[]{:S(2)}) collective-permute-start(bf16[8,64,512]{2,1,0:T(8,128)(2,1)} %get-tuple-element.20.refs_1_), channel_id=1, source_target_pairs={{0,128},{8,136},{16,144},{24,152},{32,160},{40,168},{48,176},{56,1... | collective-permute-start | bytes 1572872 | tf_op jit(solution)/shard_map/ppermute | solution.py:230
  88.3 1.9 %collective-permute-start.9 = (bf16[8,64,512]{2,1,0:T(8,128)(2,1)}, bf16[8,64,512]{2,1,0:T(8,128)(2,1)}, u32[]{:S(2)}, u32[]{:S(2)}) collective-permute-start(bf16[8,64,512]{2,1,0:T(8,128)(2,1)} %get-tuple-element.19.refs_0_), channel_id=1, source_target_pairs={{0,384},{8,392},{16,400},{24,408},{32,416},{40,424},{48,432},{56,4... | collective-permute-start | bytes 1572872 | tf_op jit(solution)/shard_map/ppermute | solution.py:230
  90.3 4.7 %collective-permute-done.7.refs_2_ = bf16[8,64,512]{2,1,0:T(8,128)(2,1)} collective-permute-done((bf16[8,64,512]{2,1,0:T(8,128)(2,1)}, bf16[8,64,512]{2,1,0:T(8,128)(2,1)}, u32[]{:S(2)}, u32[]{:S(2)}) %collective-permute-start.7) | collective-permute-done | bytes 524320 | tf_op jit(solution)/shard_map/ppermute | solution.py:230
  94.9 4.6 %collective-permute-start.11 = (bf16[8,64,512]{2,1,0:T(8,128)(2,1)}, bf16[8,64,512]{2,1,0:T(8,128)(2,1)S(1)}, u32[]{:S(2)}, u32[]{:S(2)}) collective-permute-start(bf16[8,64,512]{2,1,0:T(8,128)(2,1)} %collective-permute-done.7.refs_2_), channel_id=1, source_target_pairs={{0,128},{8,136},{16,144},{24,152},{32,160},{40,168},{48,176},{56,1... | collective-permute-start | bytes 1572872 | tf_op jit(solution)/shard_map/ppermute | solution.py:230
  101.5 4.7 %collective-permute-done.8.refs_3_ = bf16[8,64,512]{2,1,0:T(8,128)(2,1)} collective-permute-done((bf16[8,64,512]{2,1,0:T(8,128)(2,1)}, bf16[8,64,512]{2,1,0:T(8,128)(2,1)}, u32[]{:S(2)}, u32[]{:S(2)}) %collective-permute-start.8) | collective-permute-done | bytes 524320 | tf_op jit(solution)/shard_map/ppermute | solution.py:230
  106.2 4.6 %collective-permute-done.9.refs_4_ = bf16[8,64,512]{2,1,0:T(8,128)(2,1)} collective-permute-done((bf16[8,64,512]{2,1,0:T(8,128)(2,1)}, bf16[8,64,512]{2,1,0:T(8,128)(2,1)}, u32[]{:S(2)}, u32[]{:S(2)}) %collective-permute-start.9) | collective-permute-done | bytes 524320 | tf_op jit(solution)/shard_map/ppermute | solution.py:230
  110.8 3.6 %shard_map.62.total_ref = f32[512,1024]{1,0:T(8,128)S(1)} custom-call(s32[1]{0:T(128)} %bitcast.place_ref, bf16[4,2,4,64,512]{4,3,2,1,0:T(8,128)(2,1)S(1)} %all-to-all-done.2.tokens_ref, bf16[8,64,512]{2,1,0:T(8,128)(2,1)} %get-tuple-element.19.refs_0_, bf16[8,64,512]{2,1,0:T(8,128)(2,1)} %get-tuple-element.20.refs_1_, ...), custom_call_target="tpu_custom_call" | custom-call | flops 8589934592 | bytes 4194304 | tf_op jit(solution)/shard_map/pallas_call | solution.py:29
  114.5 2.9 %collective-permute-done.12.second_ref = bf16[8,64,512]{2,1,0:T(8,128)(2,1)S(1)} collective-permute-done((bf16[8,64,512]{2,1,0:T(8,128)(2,1)}, bf16[8,64,512]{2,1,0:T(8,128)(2,1)S(1)}, u32[]{:S(2)}, u32[]{:S(2)}) %collective-permute-start.12) | collective-permute-done | bytes 524320 | tf_op jit(solution)/shard_map/ppermute | solution.py:230
  118.1 1.9 %collective-permute-start.13 = (bf16[256,1024]{1,0:T(8,128)(2,1)S(1)}, bf16[256,1024]{1,0:T(8,128)(2,1)S(1)}, u32[]{:S(2)}, u32[]{:S(2)}) collective-permute-start(bf16[256,1024]{1,0:T(8,128)(2,1)S(1)} %get-tuple-element.22), channel_id=1, source_target_pairs={{0,1},{1,0},{2,3},{3,2},{4,5},{5,4},{6,7},{7,6},{8,9},{9,8},{10,11... | collective-permute-start | bytes 1572872 | tf_op jit(solution)/shard_map/ppermute | solution.py:287
  122.0 13.2 %all_to_all.20.parts_ref = bf16[4,64,1024]{2,1,0:T(8,128)(2,1)S(1)} all-to-all(bf16[4,64,1024]{2,1,0:T(8,128)(2,1)S(1)} %bitcast.8), channel_id=1, replica_groups={{0,2,4,6},{1,3,5,7},{8,10,12,14},{9,11,13,15},{16,18,20,22},{17,19,21,2..., dimensions={0} | all-to-all | bytes 1048576 | tf_op jit(solution)/shard_map/all_to_all | solution.py:289
  (31 shorter events, 10.9 us)
Async XLA Ops:
  0.0 26.3 %collective-permute-start = (bf16[64,512]{1,0:T(8,128)(2,1)}, bf16[64,512]{1,0:T(8,128)(2,1)S(1)}, u32[]{:S(2)}, u32[]{:S(2)}) collective-permute-start(bf16[64,512]{1,0:T(8,128)(2,1)} %bitcast.12), channel_id=1, source_target_pairs={{0,0},{1,1},{2,128},{3,129},{4,256},{5,257},{6,384},{7,385},{8,8},... | collective-permute-start | bytes 196616 | tf_op jit(solution)/shard_map/ppermute | solution.py:220
  7.2 41.1 %all-to-all-start = ((bf16[64,8,128]{2,1,0:T(8,128)(2,1)}), bf16[64,8,128]{2,1,0:T(8,128)(2,1)S(1)}, u32[]{:S(2)}, u32[]{:S(2)}) async-start(bf16[64,8,128]{2,1,0:T(8,128)(2,1)} %bitcast.11), calls=%async_computation | async-start | bytes 262144 | tf_op jit(solution)/shard_map/all_to_all | solution.py:249
  26.3 28.2 %collective-permute-start.1 = (bf16[64,512]{1,0:T(8,128)(2,1)S(1)}, bf16[64,512]{1,0:T(8,128)(2,1)S(1)}, u32[]{:S(2)}, u32[]{:S(2)}) collective-permute-start(bf16[64,512]{1,0:T(8,128)(2,1)S(1)} %shard_map.59.refs_0_), channel_id=1, source_target_pairs={{0,32},{8,40},{16,48},{24,56},{32,64},{40,72},{48,80},{56,88},{64,... | collective-permute-start | bytes 196616 | tf_op jit(solution)/shard_map/ppermute | solution.py:225
  33.6 20.9 %collective-permute-start.2 = (bf16[64,512]{1,0:T(8,128)(2,1)S(1)}, bf16[64,512]{1,0:T(8,128)(2,1)S(1)}, u32[]{:S(2)}, u32[]{:S(2)}) collective-permute-start(bf16[64,512]{1,0:T(8,128)(2,1)S(1)} %shard_map.59.refs_0_), channel_id=1, source_target_pairs={{0,96},{8,104},{16,112},{24,120},{32,0},{40,8},{48,16},{56,24},{64... | collective-permute-start | bytes 196616 | tf_op jit(solution)/shard_map/ppermute | solution.py:225
  36.1 18.5 %collective-permute-start.3 = (bf16[64,512]{1,0:T(8,128)(2,1)S(1)}, bf16[64,512]{1,0:T(8,128)(2,1)S(1)}, u32[]{:S(2)}, u32[]{:S(2)}) collective-permute-start(bf16[64,512]{1,0:T(8,128)(2,1)S(1)} %shard_map.59.refs_0_), channel_id=1, source_target_pairs={{0,64},{8,72},{16,80},{24,88},{32,96},{40,104},{48,112},{56,120},{... | collective-permute-start | bytes 196616 | tf_op jit(solution)/shard_map/ppermute | solution.py:225
  49.0 20.6 %all-to-all-start.1 = ((bf16[64,8,128]{2,1,0:T(8,128)(2,1)}), bf16[64,8,128]{2,1,0:T(8,128)(2,1)S(1)}, u32[]{:S(2)}, u32[]{:S(2)}) async-start(bf16[64,8,128]{2,1,0:T(8,128)(2,1)} %shard_map.56), calls=%async_computation.1 | async-start | bytes 262144 | tf_op jit(solution)/shard_map/all_to_all | solution.py:253
  54.5 15.1 %copy-start = (bf16[512,512]{1,0:T(8,128)(2,1)S(1)}, bf16[512,512]{1,0:T(8,128)(2,1)}, u32[]{:S(2)}) copy-start(bf16[512,512]{1,0:T(8,128)(2,1)} %values_ref.3) | copy-start | bytes 1572868
  54.5 15.1 %copy-start.1 = (bf16[512,512]{1,0:T(8,128)(2,1)S(1)}, bf16[512,512]{1,0:T(8,128)(2,1)}, u32[]{:S(2)}) copy-start(bf16[512,512]{1,0:T(8,128)(2,1)} %queries_ref) | copy-start | bytes 1572868
  54.5 15.0 %copy-start.2 = (bf16[512,512]{1,0:T(8,128)(2,1)S(1)}, bf16[512,512]{1,0:T(8,128)(2,1)}, u32[]{:S(2)}) copy-start(bf16[512,512]{1,0:T(8,128)(2,1)} %get-tuple-element.16.key_ref) | copy-start | bytes 1572868
  54.5 16.5 %copy-start.3 = (f32[512]{0:T(512)S(1)}, f32[512]{0:T(512)}, u32[]{:S(2)}) copy-start(f32[512]{0:T(512)} %param.9) | copy-start | bytes 6148
  54.6 22.2 %collective-permute-start.4 = (bf16[4,64,512]{2,1,0:T(8,128)(2,1)S(1)}, bf16[4,64,512]{2,1,0:T(8,128)(2,1)S(1)}, u32[]{:S(2)}, u32[]{:S(2)}) collective-permute-start(bf16[4,64,512]{2,1,0:T(8,128)(2,1)S(1)} %shard_map.60.refs_0_), channel_id=1, source_target_pairs={{0,8},{8,16},{16,24},{24,32},{32,40},{40,48},{48,56},{56,64},{64,7... | collective-permute-start | bytes 786440 | tf_op jit(solution)/shard_map/ppermute | solution.py:225
  58.1 18.7 %collective-permute-start.5 = (bf16[4,64,512]{2,1,0:T(8,128)(2,1)S(1)}, bf16[4,64,512]{2,1,0:T(8,128)(2,1)S(1)}, u32[]{:S(2)}, u32[]{:S(2)}) collective-permute-start(bf16[4,64,512]{2,1,0:T(8,128)(2,1)S(1)} %shard_map.60.refs_0_), channel_id=1, source_target_pairs={{0,120},{8,0},{16,8},{24,16},{32,24},{40,32},{48,40},{56,48},{64,5... | collective-permute-start | bytes 786440 | tf_op jit(solution)/shard_map/ppermute | solution.py:225
  62.1 14.7 %collective-permute-start.6 = (bf16[4,64,512]{2,1,0:T(8,128)(2,1)S(1)}, bf16[4,64,512]{2,1,0:T(8,128)(2,1)S(1)}, u32[]{:S(2)}, u32[]{:S(2)}) collective-permute-start(bf16[4,64,512]{2,1,0:T(8,128)(2,1)S(1)} %shard_map.60.refs_0_), channel_id=1, source_target_pairs={{0,16},{8,120},{16,32},{24,8},{32,48},{40,24},{48,64},{56,40},{64,... | collective-permute-start | bytes 786440 | tf_op jit(solution)/shard_map/ppermute | solution.py:225
  73.1 37.7 %all-to-all-start.2 = ((bf16[4,2,4,64,512]{4,3,2,1,0:T(8,128)(2,1)}), bf16[4,2,4,64,512]{4,3,2,1,0:T(8,128)(2,1)S(1)}, u32[]{:S(2)}, u32[]{:S(2)}) async-start(bf16[4,2,4,64,512]{4,3,2,1,0:T(8,128)(2,1)} %broadcast_in_dim.2), calls=%async_computation.2 | async-start | bytes 4194304 | tf_op jit(solution)/shard_map/all_to_all | solution.py:273
  77.9 17.1 %collective-permute-start.7 = (bf16[8,64,512]{2,1,0:T(8,128)(2,1)}, bf16[8,64,512]{2,1,0:T(8,128)(2,1)}, u32[]{:S(2)}, u32[]{:S(2)}) collective-permute-start(bf16[8,64,512]{2,1,0:T(8,128)(2,1)} %get-tuple-element.19.refs_0_), channel_id=1, source_target_pairs={{0,128},{8,136},{16,144},{24,152},{32,160},{40,168},{48,176},{56,1... | collective-permute-start | bytes 1572872 | tf_op jit(solution)/shard_map/ppermute | solution.py:230
  81.3 18.3 %collective-permute-start.10 = (bf16[8,64,512]{2,1,0:T(8,128)(2,1)}, bf16[8,64,512]{2,1,0:T(8,128)(2,1)}, u32[]{:S(2)}, u32[]{:S(2)}) collective-permute-start(bf16[8,64,512]{2,1,0:T(8,128)(2,1)} %get-tuple-element.20.refs_1_), channel_id=1, source_target_pairs={{0,384},{8,392},{16,400},{24,408},{32,416},{40,424},{48,432},{56,4... | collective-permute-start | bytes 1572872 | tf_op jit(solution)/shard_map/ppermute | solution.py:230
  83.7 22.4 %collective-permute-start.8 = (bf16[8,64,512]{2,1,0:T(8,128)(2,1)}, bf16[8,64,512]{2,1,0:T(8,128)(2,1)}, u32[]{:S(2)}, u32[]{:S(2)}) collective-permute-start(bf16[8,64,512]{2,1,0:T(8,128)(2,1)} %get-tuple-element.20.refs_1_), channel_id=1, source_target_pairs={{0,128},{8,136},{16,144},{24,152},{32,160},{40,168},{48,176},{56,1... | collective-permute-start | bytes 1572872 | tf_op jit(solution)/shard_map/ppermute | solution.py:230
  88.3 22.4 %collective-permute-start.9 = (bf16[8,64,512]{2,1,0:T(8,128)(2,1)}, bf16[8,64,512]{2,1,0:T(8,128)(2,1)}, u32[]{:S(2)}, u32[]{:S(2)}) collective-permute-start(bf16[8,64,512]{2,1,0:T(8,128)(2,1)} %get-tuple-element.19.refs_0_), channel_id=1, source_target_pairs={{0,384},{8,392},{16,400},{24,408},{32,416},{40,424},{48,432},{56,4... | collective-permute-start | bytes 1572872 | tf_op jit(solution)/shard_map/ppermute | solution.py:230
  94.9 19.5 %collective-permute-start.11 = (bf16[8,64,512]{2,1,0:T(8,128)(2,1)}, bf16[8,64,512]{2,1,0:T(8,128)(2,1)S(1)}, u32[]{:S(2)}, u32[]{:S(2)}) collective-permute-start(bf16[8,64,512]{2,1,0:T(8,128)(2,1)} %collective-permute-done.7.refs_2_), channel_id=1, source_target_pairs={{0,128},{8,136},{16,144},{24,152},{32,160},{40,168},{48,176},{56,1... | collective-permute-start | bytes 1572872 | tf_op jit(solution)/shard_map/ppermute | solution.py:230
  99.6 17.8 %collective-permute-start.12 = (bf16[8,64,512]{2,1,0:T(8,128)(2,1)}, bf16[8,64,512]{2,1,0:T(8,128)(2,1)S(1)}, u32[]{:S(2)}, u32[]{:S(2)}) collective-permute-start(bf16[8,64,512]{2,1,0:T(8,128)(2,1)} %collective-permute-done.10.refs_5_), channel_id=1, source_target_pairs={{0,384},{8,392},{16,400},{24,408},{32,416},{40,424},{48,432},{56,4... | collective-permute-start | bytes 1572872 | tf_op jit(solution)/shard_map/ppermute | solution.py:230
  118.1 3.8 %collective-permute-start.13 = (bf16[256,1024]{1,0:T(8,128)(2,1)S(1)}, bf16[256,1024]{1,0:T(8,128)(2,1)S(1)}, u32[]{:S(2)}, u32[]{:S(2)}) collective-permute-start(bf16[256,1024]{1,0:T(8,128)(2,1)S(1)} %get-tuple-element.22), channel_id=1, source_target_pairs={{0,1},{1,0},{2,3},{3,2},{4,5},{5,4},{6,7},{7,6},{8,9},{9,8},{10,11... | collective-permute-start | bytes 1572872 | tf_op jit(solution)/shard_map/ppermute | solution.py:287
